TPU v7x, 128 devices: a whole 4x4x4 slice. The times are simulated.
128 devices in a mesh: ma: 8 (over y, x_hi), blk: 16 (over x_lo, z, core).
Axes of the slice: x: 4 (x_hi: 2, x_lo: 2; x = x_hi * 2 + x_lo), y: 4, z: 4, core: 2. Of those that a mesh axis runs over, the one named last changes fastest.
Arguments:
- cycle_rows: float32 [65536, 2048], P(('ma', 'blk')), may hold values from -6 to 6
- owner_map: int32 [16], replicated, may hold values from 0 to 15, each once
- factors: float32 [4, 16, 1024, 64, 128], P(None, 'ma', 'blk'), may hold values from -0.5 to 0.5
Outputs:
- coeffs: float32 [16, 1024, 64, 128], P('ma', 'blk')
Inputs may be any that keep to these rules, and one draw needn't show every extreme that they name: owner_map is a permutation of the m-blocks; slot q of factors and of coeffs belongs to m-block owner_map[q].
All inputs are finite; a program needn't handle non-finite values.
Results may differ from a plain program's by a relative error of at most 0.0001.
Values sent between devices are 32-bit elements; how exact they have to be, the bound alone decides.
No kernel may reach another device: no remote copies, remote signals or barrier semaphores. Data moves between devices by JAX's collectives and lax.ppermute only.
A program may use at most 128 MiB of HBM per device.

v0:
```python
import collections
import functools

import jax
import jax.numpy as jnp
from jax import lax
from jax.experimental import pallas as pl
from jax.experimental.pallas import tpu as pltpu
from jax.sharding import PartitionSpec as P

ANY = pl.BlockSpec(memory_space=pl.ANY)
VMEM = pl.BlockSpec(memory_space=pltpu.VMEM)
SCALARS = pl.BlockSpec(memory_space=pltpu.SMEM)
MARK = pltpu.VMEM((8, 128), jnp.float32)
FREE = pl.CostEstimate(flops=0, bytes_accessed=0, transcendentals=0)
PARAMS = pltpu.CompilerParams(vmem_limit_bytes=4 << 20)

Chunk = collections.namedtuple("Chunk", ["part", "slot", "slots", "group", "groups"])


def permute_xor(x, axis, mask):
    return lax.ppermute(x, axis, [(i, i ^ mask) for i in range(lax.axis_size(axis))])


def in_vmem(x):
    return pltpu.with_memory_space_constraint(x, pltpu.VMEM)


def in_hbm(x):
    return pltpu.with_memory_space_constraint(x, pltpu.HBM)


def call(body, operands, in_specs, outs, out_specs, token, name, scratch=(), aliases={}):
    tokens = [] if token is None else [token]
    return pl.pallas_call(
        body,
        in_specs=in_specs + [ANY] * len(tokens),
        out_specs=out_specs + [ANY],
        out_shape=outs + [MARK],
        scratch_shapes=list(scratch),
        input_output_aliases=aliases,
        cost_estimate=FREE,
        compiler_params=PARAMS,
        name=name,
    )(*operands, *tokens)


def run_copies(copies):
    for copy in copies:
        copy.start()
    for copy in copies:
        copy.wait()


def pick_body(chunks, local_slots, place, owner_map, rows, *refs):
    outs, sems = refs[-2 - len(chunks) : -2], refs[-1]
    copies = []
    for chunk, out in zip(chunks, outs):
        cols = out.shape[-1]
        for slot in range(chunk.slots):
            column = owner_map[(place[0] ^ chunk.part) * local_slots + chunk.slot + slot]
            start = pl.multiple_of(column * cols, cols)
            source = rows.at[pl.ds(chunk.group, chunk.groups), :, pl.ds(start, cols)]
            copies.append(pltpu.make_async_copy(source, out.at[slot], sems.at[len(copies)]))
    run_copies(copies)


def pick_slots(place, owner_map, rows, chunks, local_slots, block_cols, token):
    outs = [
        pltpu.VMEM((chunk.slots, chunk.groups, rows.shape[1], block_cols), rows.dtype)
        for chunk in chunks
    ]
    return call(
        functools.partial(pick_body, chunks, local_slots),
        [place, owner_map, in_hbm(rows)],
        [SCALARS, SCALARS, ANY],
        outs,
        [VMEM] * len(chunks),
        token,
        "pick_slots",
        [pltpu.SemaphoreType.DMA((sum(chunk.slots for chunk in chunks),))],
    )


def fetch_body(level, factors, *refs):
    out, sems = refs[-3], refs[-1]
    run_copies(
        [
            pltpu.make_async_copy(factors.at[level, slot], out.at[slot], sems.at[slot])
            for slot in range(out.shape[0])
        ]
    )


def fetch_factors(factors, level, token):
    return call(
        functools.partial(fetch_body, level),
        [in_hbm(factors)],
        [ANY],
        [pltpu.VMEM(factors.shape[1:], factors.dtype)],
        [VMEM],
        token,
        "fetch_factors",
        [pltpu.SemaphoreType.DMA((factors.shape[1],))],
    )


def borrow_body(level, chunk, parts, place, factors, *refs):
    out, sem = refs[-3], refs[-1]
    first = (place[0] ^ chunk.part) * (factors.shape[2] // parts) + chunk.group
    source = factors.at[level, pl.ds(chunk.slot, chunk.slots), pl.ds(first, chunk.groups)]
    run_copies([pltpu.make_async_copy(source, out, sem)])


def pick_factors(place, factors, level, chunk, parts, token):
    shape = (chunk.slots, chunk.groups) + factors.shape[3:]
    return call(
        functools.partial(borrow_body, level, chunk, parts),
        [place, in_hbm(factors)],
        [SCALARS, ANY],
        [pltpu.VMEM(shape, factors.dtype)],
        [VMEM],
        token,
        "pick_factors",
        [pltpu.SemaphoreType.DMA],
    )


def gate_body(x, *refs):
    pass


def gate(x, token):
    return call(
        gate_body,
        [in_vmem(x)],
        [ANY],
        [pltpu.VMEM(x.shape, x.dtype)],
        [ANY],
        token,
        "gate",
        aliases={0: 0},
    )


def split(x):
    high = x.astype(jnp.bfloat16)
    return high, (x - high.astype(jnp.float32)).astype(jnp.bfloat16)


def block_product(factor, own, other):
    factor_high, factor_low = split(factor)
    high, low = split(jnp.concatenate([own, other], axis=0))
    dot = functools.partial(jnp.dot, preferred_element_type=jnp.float32)
    both = jnp.concatenate([factor_high, factor_low], axis=1)
    return dot(both, jnp.concatenate([high, high], axis=0)) + dot(factor_high, low)


def early_body(chunk, parts, place, factors, own, other, *refs):
    out, held, sem = refs[-4], refs[-2], refs[-1]
    first = (place[0] ^ chunk.part) * (factors.shape[2] // parts) + chunk.group
    source = factors.at[0, pl.ds(chunk.slot, chunk.slots), pl.ds(first, chunk.groups)]
    run_copies([pltpu.make_async_copy(source, held, sem)])
    for slot in range(chunk.slots):
        for group in range(chunk.groups):
            out[slot, group] = block_product(held[slot, group], own[slot, group], other[slot, group])


def early_product(place, factors, own, other, chunk, parts, token):
    held = own.shape[:3] + factors.shape[4:]
    return call(
        functools.partial(early_body, chunk, parts),
        [place, in_hbm(factors), in_vmem(own), in_vmem(other)],
        [SCALARS, ANY, VMEM, VMEM],
        [pltpu.VMEM(own.shape, own.dtype)],
        [VMEM],
        token,
        "early_product",
        [pltpu.VMEM(held, factors.dtype), pltpu.SemaphoreType.DMA],
    )


def level_body(chunk, parts, place, factors, own, other, *refs):
    out = refs[-2]
    first = (place[0] ^ chunk.part) * (factors.shape[1] // parts) + chunk.group
    for slot in range(chunk.slots):
        for group in range(chunk.groups):
            factor = factors[chunk.slot + slot, first + group]
            out[slot, group] = block_product(factor, own[slot, group], other[slot, group])


def level_product(place, factors, own, other, chunk, parts, token):
    return call(
        functools.partial(level_body, chunk, parts),
        [place, in_vmem(factors), in_vmem(own), in_vmem(other)],
        [SCALARS, VMEM, VMEM, VMEM],
        [pltpu.VMEM(own.shape, own.dtype)],
        [VMEM],
        token,
        "level_product",
    )


def both_body(chunk, parts, place, factors, lent, own, other, *refs):
    out, partner_out = refs[-3], refs[-2]
    first = (place[0] ^ chunk.part) * (factors.shape[1] // parts) + chunk.group
    for slot in range(chunk.slots):
        for group in range(chunk.groups):
            factor = factors[chunk.slot + slot, first + group]
            mine, theirs = own[slot, group], other[slot, group]
            out[slot, group] = block_product(factor, mine, theirs)
            partner_out[slot, group] = block_product(lent[slot, group], theirs, mine)


def both_products(place, factors, lent, own, other, chunk, parts, token):
    shape = pltpu.VMEM(own.shape, own.dtype)
    return call(
        functools.partial(both_body, chunk, parts),
        [place, in_vmem(factors), in_vmem(lent), in_vmem(own), in_vmem(other)],
        [SCALARS, VMEM, VMEM, VMEM, VMEM],
        [shape, shape],
        [VMEM, VMEM],
        token,
        "both_products",
    )


def last_body(chunk, parts, place, factors, own, other, *refs):
    out, held, sem = refs[-4], refs[-2], refs[-1]
    first = (place[0] ^ chunk.part) * (factors.shape[1] // parts) + chunk.group
    for slot in range(chunk.slots):
        for group in range(chunk.groups):
            factor = factors[chunk.slot + slot, first + group]
            held[slot, group] = block_product(factor, own[slot, group], other[slot, group])
    place_out = out.at[pl.ds(chunk.slot, chunk.slots), pl.ds(first, chunk.groups)]
    run_copies([pltpu.make_async_copy(held, place_out, sem)])


def last_product(place, factors, own, other, chunk, parts, token, coeffs):
    filled = [] if coeffs is None else [in_hbm(coeffs)]
    return call(
        functools.partial(last_body, chunk, parts),
        [place, in_vmem(factors), in_vmem(own), in_vmem(other)] + filled,
        [SCALARS, VMEM, VMEM, VMEM] + [ANY] * len(filled),
        [pltpu.HBM(factors.shape[:3] + own.shape[3:], own.dtype)],
        [ANY],
        token,
        "last_product",
        [pltpu.VMEM(own.shape, own.dtype), pltpu.SemaphoreType.DMA],
        {4: 0} if filled else {},
    )


ORDER = (0, 2, 1, 6, 3, 4, 7, 5)
CUTS = {5: (2, 2)}

PICK, LAND, SEND, FETCH, LEND = range(5)
PLAN = (
    (PICK, 0), (LEND, 0), (PICK, 1), (PICK, 2), LAND, (SEND, 0), (PICK, 3), LAND, (FETCH, 1), LAND, (LEND, 1),
    (PICK, 4), LAND, (FETCH, 0), (FETCH, 3), LAND, LAND, LAND, (SEND, 1), (FETCH, 2), LAND, (PICK, 5), LAND,
    LAND, (SEND, 2), LAND, LAND, LAND, (SEND, 3), LAND, LAND, (PICK, 6), LAND, LAND, LAND, (PICK, 7),
    (SEND, 4), LAND, LAND, LAND, LAND, (SEND, 5), (PICK, 8), LAND, LAND, LAND, LAND, LAND, (SEND, 6), LAND,
    LAND, LAND, LAND, LAND, LAND, (SEND, 7), LAND, LAND, LAND, LAND, (SEND, 8), LAND, LAND, LAND, LAND, LAND,
    LAND, LAND, LAND, LAND,
)


def pieces(part, slots, groups, sizes):
    cut, slot, group = [], 0, 0
    for size in sizes:
        blocks = slots * groups // size
        if blocks == slots * groups:
            return [Chunk(part, 0, slots, 0, groups)]
        cut.append(Chunk(part, slot, 1, group, blocks))
        slot, group = (slot, group + blocks) if group + blocks < groups else (slot + 1, 0)
    return cut


def chunks_of(parts, slots, groups):
    cut = []
    for part in ORDER:
        cut += pieces(part, slots, groups, CUTS.get(part, (1,)))
    return cut


def on_device(cycle_rows, owner_map, factors):
    block_count = owner_map.shape[0]
    block_cols = cycle_rows.shape[1] // block_count
    level_count, local_slots, group_count, rank, _ = factors.shape
    parts = lax.axis_size("ma")
    bit_count = lax.axis_size("blk").bit_length() - 1
    place = jnp.reshape(lax.axis_index("ma"), (1,)).astype(jnp.int32)
    groups = group_count // parts
    rows = cycle_rows.reshape(groups, rank, cycle_rows.shape[1])
    chunks = chunks_of(parts, local_slots, groups)
    state, other, fetched, lent = {}, {}, {}, {}
    token, coeffs = None, None
    flying = collections.deque()

    def exchange(i, level):
        other[i] = permute_xor(state[i], "blk", 1 << (level % bit_count))
        flying.append((level, i))

    def fetch(level):
        nonlocal token
        if level not in fetched:
            fetched[level], token = fetch_factors(factors, level, token)
        return fetched[level]

    def pick(i):
        nonlocal token
        state[i], token = pick_slots(
            place, owner_map, rows, [chunks[i]], local_slots, block_cols, token
        )
        if chunks[i].part:
            state[i] = permute_xor(state[i], "ma", chunks[i].part)
            flying.append((-1, i))
        else:
            exchange(i, 0)

    def lend(i):
        nonlocal token
        lent[i], token = pick_factors(place, factors, 1, chunks[i], parts, token)
        lent[i] = permute_xor(lent[i], "blk", 1 << (1 % bit_count))
        flying.append((-2, i))

    def land(level, i):
        nonlocal token, coeffs
        if level == -2:
            lent[i], token = gate(lent[i], token)
            return
        if level == 1 and i in lent:
            state[i], theirs, token = both_products(
                place, fetch(1), lent.pop(i), state[i], other[i], chunks[i], parts, token
            )
            bits = (1 << (1 % bit_count)) ^ (1 << (2 % bit_count))
            other[i] = permute_xor(theirs, "blk", bits)
            flying.append((2, i))
            return
        if level < 0:
            state[i], token = gate(state[i], token)
        elif level == 0 and not chunks[i].part:
            state[i], token = early_product(
                place, factors, state[i], other[i], chunks[i], parts, token
            )
        elif level < level_count - 1:
            state[i], token = level_product(
                place, fetch(level), state[i], other[i], chunks[i], parts, token
            )
        else:
            coeffs, token = last_product(
                place, fetch(level), state[i], other[i], chunks[i], parts, token, coeffs
            )
            return
        if level == 0:
            ready.append(i)
        else:
            exchange(i, level + 1)

    def send(i):
        nonlocal token
        if ready[-1] != i or not fresh:
            state[i], token = gate(state[i], token)
        ready.remove(i)
        exchange(i, 1)

    ready, fresh = [], False
    for step in PLAN:
        if step == LAND:
            level, i = flying.popleft()
            land(level, i)
            fresh = level == 0
        else:
            what, i = step
            {PICK: pick, SEND: send, FETCH: fetch, LEND: lend}[what](i)
            fresh = False
    return coeffs


def solution(mesh):
    placed = (P(("ma", "blk"), None), P(), P(None, "ma", "blk", None, None))
    return jax.shard_map(
        on_device, mesh=mesh, in_specs=placed, out_specs=P("ma", "blk", None, None), check_vma=False
    )
```

profile of v0, /device:TPU:0, one launch (start us, length us, event | category | flops | bytes accessed | tf_op | source)
XLA Modules:
  0.0 201.4 jit_solution(14421505646579573637)
XLA Ops:
  0.7 1.6 pick_slots.9
  3.4 2.1 %collective-permute-start.2 = (f32[2,8,64,128]{3,2,1,0:T(8,128)S(1)}, f32[2,8,64,128]{3,2,1,0:T(8,128)S(1)}, u32[]{:S(2)}, u32[]{:S(2)}) collective-permute-start(f32[2,8,64,128]{3,2,1,0:T(8,128)S(1)} %get-tuple-element.143), channel_id=1, source_target_pairs={{0,2},{1,3},{2,0},{3,1},{4,6},{5,7},{6,4},{7,5},{8,10},{9,11},{10,... | collective-permute-start | bytes 1572872 | tf_op jit(solution)/shard_map/ppermute | solution.py:22
  5.5 1.6 pick_slots.10
  7.1 1.7 collective-permute-start.1
  8.8 1.6 pick_slots.11
  10.4 3.1 %collective-permute-start = (f32[2,8,64,128]{3,2,1,0:T(8,128)S(1)}, f32[2,8,64,128]{3,2,1,0:T(8,128)S(1)}, u32[]{:S(2)}, u32[]{:S(2)}) collective-permute-start(f32[2,8,64,128]{3,2,1,0:T(8,128)S(1)} %get-tuple-element.141), channel_id=1, source_target_pairs={{0,16},{16,0},{32,48},{48,32},{64,80},{80,64},{96,112},{112,96},{1... | collective-permute-start | bytes 1572872 | tf_op jit(solution)/shard_map/ppermute | solution.py:22
  15.2 1.6 pick_slots.12
  16.8 2.3 %collective-permute-start.5 = (f32[2,8,64,128]{3,2,1,0:T(8,128)S(1)}, f32[2,8,64,128]{3,2,1,0:T(8,128)S(1)}, u32[]{:S(2)}, u32[]{:S(2)}) collective-permute-start(f32[2,8,64,128]{3,2,1,0:T(8,128)S(1)} %get-tuple-element.158), channel_id=1, source_target_pairs={{0,96},{16,112},{32,64},{48,80},{64,32},{80,48},{96,0},{112,16},{1... | collective-permute-start | bytes 1572872 | tf_op jit(solution)/shard_map/ppermute | solution.py:22
  19.0 2.2 %fetch_factors.4 = (f32[2,64,64,128]{3,2,1,0:T(8,128)S(1)}, f32[8,128]{1,0:T(8,128)S(1)}) custom-call(f32[4,2,64,64,128]{4,3,2,1,0:T(8,128)} %factors.13, f32[8,128]{1,0:T(8,128)S(1)} %get-tuple-element.148.refs_0_), custom_call_target="tpu_custom_call" | custom-call | tf_op jit(solution)/shard_map/fetch_factors/pallas_call | solution.py:35
  22.4 2.0 collective-permute-start.7
  24.4 1.6 pick_slots.13
  26.0 3.4 %collective-permute-start.12 = (f32[2,8,64,128]{3,2,1,0:T(8,128)S(1)}, f32[2,8,64,128]{3,2,1,0:T(8,128)S(1)}, u32[]{:S(2)}, u32[]{:S(2)}) collective-permute-start(f32[2,8,64,128]{3,2,1,0:T(8,128)S(1)} %get-tuple-element.175), channel_id=1, source_target_pairs={{0,48},{16,32},{32,16},{48,0},{64,112},{80,96},{96,80},{112,64},{1... | collective-permute-start | bytes 1572872 | tf_op jit(solution)/shard_map/ppermute | solution.py:22
  29.5 2.2 %fetch_factors.5 = (f32[2,64,64,128]{3,2,1,0:T(8,128)S(1)}, f32[8,128]{1,0:T(8,128)S(1)}) custom-call(f32[4,2,64,64,128]{4,3,2,1,0:T(8,128)} %factors.13, f32[8,128]{1,0:T(8,128)S(1)} %get-tuple-element.153.refs_0_), custom_call_target="tpu_custom_call" | custom-call | tf_op jit(solution)/shard_map/fetch_factors/pallas_call | solution.py:35
  31.7 2.2 %fetch_factors.6 = (f32[2,64,64,128]{3,2,1,0:T(8,128)S(1)}, f32[8,128]{1,0:T(8,128)S(1)}) custom-call(f32[4,2,64,64,128]{4,3,2,1,0:T(8,128)} %factors.13, f32[8,128]{1,0:T(8,128)S(1)} %get-tuple-element.154.refs_0_), custom_call_target="tpu_custom_call" | custom-call | tf_op jit(solution)/shard_map/fetch_factors/pallas_call | solution.py:35
  34.8 2.9 %collective-permute-start.10 = (f32[2,8,64,128]{3,2,1,0:T(8,128)S(1)}, f32[2,8,64,128]{3,2,1,0:T(8,128)S(1)}, u32[]{:S(2)}, u32[]{:S(2)}) collective-permute-start(f32[2,8,64,128]{3,2,1,0:T(8,128)S(1)} %get-tuple-element.173), channel_id=1, source_target_pairs={{0,6},{1,7},{2,4},{3,5},{4,2},{5,3},{6,0},{7,1},{8,14},{9,15},{10,... | collective-permute-start | bytes 1572872 | tf_op jit(solution)/shard_map/ppermute | solution.py:22
  38.3 2.3 %collective-permute-done.7.x = f32[2,8,64,128]{3,2,1,0:T(8,128)S(1)} collective-permute-done((f32[2,8,64,128]{3,2,1,0:T(8,128)S(1)}, f32[2,8,64,128]{3,2,1,0:T(8,128)S(1)}, u32[]{:S(2)}, u32[]{:S(2)}) %collective-permute-start.7) | collective-permute-done | bytes 524320 | tf_op jit(solution)/shard_map/ppermute | solution.py:22
  40.6 1.7 collective-permute-start.13
  42.3 2.2 %fetch_factors.7 = (f32[2,64,64,128]{3,2,1,0:T(8,128)S(1)}, f32[8,128]{1,0:T(8,128)S(1)}) custom-call(f32[4,2,64,64,128]{4,3,2,1,0:T(8,128)} %factors.13, f32[8,128]{1,0:T(8,128)S(1)} %get-tuple-element.165.refs_0_), custom_call_target="tpu_custom_call" | custom-call | tf_op jit(solution)/shard_map/fetch_factors/pallas_call | solution.py:35
  44.6 1.6 pick_slots.14
  46.2 3.3 %collective-permute-start.8 = (f32[2,8,64,128]{3,2,1,0:T(8,128)S(1)}, f32[2,8,64,128]{3,2,1,0:T(8,128)S(1)}, u32[]{:S(2)}, u32[]{:S(2)}) collective-permute-start(f32[2,8,64,128]{3,2,1,0:T(8,128)S(1)} %get-tuple-element.170), channel_id=1, source_target_pairs={{0,64},{16,80},{32,96},{48,112},{64,0},{80,16},{96,32},{112,48},{1... | collective-permute-start | bytes 1572872 | tf_op jit(solution)/shard_map/ppermute | solution.py:22
  52.7 2.4 %collective-permute-done.13.other = f32[2,8,64,128]{3,2,1,0:T(8,128)S(1)} collective-permute-done((f32[2,8,64,128]{3,2,1,0:T(8,128)S(1)}, f32[2,8,64,128]{3,2,1,0:T(8,128)S(1)}, u32[]{:S(2)}, u32[]{:S(2)}) %collective-permute-start.13) | collective-permute-done | bytes 524320 | tf_op jit(solution)/shard_map/ppermute | solution.py:22
  55.8 4.3 %collective-permute-start.17 = (f32[2,8,64,128]{3,2,1,0:T(8,128)S(1)}, f32[2,8,64,128]{3,2,1,0:T(8,128)S(1)}, u32[]{:S(2)}, u32[]{:S(2)}) collective-permute-start(f32[2,8,64,128]{3,2,1,0:T(8,128)S(1)} %get-tuple-element.192), channel_id=1, source_target_pairs={{0,6},{1,7},{2,4},{3,5},{4,2},{5,3},{6,0},{7,1},{8,14},{9,15},{10,... | collective-permute-start | bytes 1572872 | tf_op jit(solution)/shard_map/ppermute | solution.py:22
  61.8 1.6 pick_slots.15
  63.4 2.9 %collective-permute-done.19.other = f32[2,8,64,128]{3,2,1,0:T(8,128)S(1)} collective-permute-done((f32[2,8,64,128]{3,2,1,0:T(8,128)S(1)}, f32[2,8,64,128]{3,2,1,0:T(8,128)S(1)}, u32[]{:S(2)}, u32[]{:S(2)}) %collective-permute-start.19) | collective-permute-done | bytes 524320 | tf_op jit(solution)/shard_map/ppermute | solution.py:22
  66.3 5.8 %collective-permute-start.21 = (f32[2,8,64,128]{3,2,1,0:T(8,128)S(1)}, f32[2,8,64,128]{3,2,1,0:T(8,128)S(1)}, u32[]{:S(2)}, u32[]{:S(2)}) collective-permute-start(f32[2,8,64,128]{3,2,1,0:T(8,128)S(1)} %get-tuple-element.205), channel_id=1, source_target_pairs={{0,112},{16,96},{32,80},{48,64},{64,48},{80,32},{96,16},{112,0},{1... | collective-permute-start | bytes 1572872 | tf_op jit(solution)/shard_map/ppermute | solution.py:22
  72.5 3.8 %collective-permute-start.20 = (f32[2,8,64,128]{3,2,1,0:T(8,128)S(1)}, f32[2,8,64,128]{3,2,1,0:T(8,128)S(1)}, u32[]{:S(2)}, u32[]{:S(2)}) collective-permute-start(f32[2,8,64,128]{3,2,1,0:T(8,128)S(1)} %get-tuple-element.204.own), channel_id=1, source_target_pairs={{0,4},{1,5},{2,6},{3,7},{4,0},{5,1},{6,2},{7,3},{8,12},{9,13},{10,... | collective-permute-start | bytes 1572872 | tf_op jit(solution)/shard_map/ppermute | solution.py:22
  80.2 3.3 %collective-permute-start.29 = (f32[1,8,64,128]{3,2,1,0:T(8,128)S(1)}, f32[1,8,64,128]{3,2,1,0:T(8,128)S(1)}, u32[]{:S(2)}, u32[]{:S(2)}) collective-permute-start(f32[1,8,64,128]{3,2,1,0:T(8,128)S(1)} %get-tuple-element.220), channel_id=1, source_target_pairs={{0,80},{16,64},{32,112},{48,96},{64,16},{80,0},{96,48},{112,32},{1... | collective-permute-start | bytes 786440 | tf_op jit(solution)/shard_map/ppermute | solution.py:22
  83.9 1.8 collective-permute-start.28
  86.2 3.7 %collective-permute-start.27 = (f32[2,8,64,128]{3,2,1,0:T(8,128)S(1)}, f32[2,8,64,128]{3,2,1,0:T(8,128)S(1)}, u32[]{:S(2)}, u32[]{:S(2)}) collective-permute-start(f32[2,8,64,128]{3,2,1,0:T(8,128)S(1)} %get-tuple-element.218.own), channel_id=1, source_target_pairs={{0,4},{1,5},{2,6},{3,7},{4,0},{5,1},{6,2},{7,3},{8,12},{9,13},{10,... | collective-permute-start | bytes 1572872 | tf_op jit(solution)/shard_map/ppermute | solution.py:22
  89.9 2.5 %collective-permute-done.20.other = f32[2,8,64,128]{3,2,1,0:T(8,128)S(1)} collective-permute-done((f32[2,8,64,128]{3,2,1,0:T(8,128)S(1)}, f32[2,8,64,128]{3,2,1,0:T(8,128)S(1)}, u32[]{:S(2)}, u32[]{:S(2)}) %collective-permute-start.20) | collective-permute-done | bytes 524320 | tf_op jit(solution)/shard_map/ppermute | solution.py:22
  92.8 6.3 %collective-permute-done.29.x = f32[1,8,64,128]{3,2,1,0:T(8,128)S(1)} collective-permute-done((f32[1,8,64,128]{3,2,1,0:T(8,128)S(1)}, f32[1,8,64,128]{3,2,1,0:T(8,128)S(1)}, u32[]{:S(2)}, u32[]{:S(2)}) %collective-permute-start.29) | collective-permute-done | bytes 262176 | tf_op jit(solution)/shard_map/ppermute | solution.py:22
  100.6 1.5 collective-permute-start.23
  105.3 3.7 %collective-permute-start.35 = (f32[2,8,64,128]{3,2,1,0:T(8,128)S(1)}, f32[2,8,64,128]{3,2,1,0:T(8,128)S(1)}, u32[]{:S(2)}, u32[]{:S(2)}) collective-permute-start(f32[2,8,64,128]{3,2,1,0:T(8,128)S(1)} %get-tuple-element.236.own), channel_id=1, source_target_pairs={{0,4},{1,5},{2,6},{3,7},{4,0},{5,1},{6,2},{7,3},{8,12},{9,13},{10,... | collective-permute-start | bytes 1572872 | tf_op jit(solution)/shard_map/ppermute | solution.py:22
  109.0 5.9 %collective-permute-done.27.other = f32[2,8,64,128]{3,2,1,0:T(8,128)S(1)} collective-permute-done((f32[2,8,64,128]{3,2,1,0:T(8,128)S(1)}, f32[2,8,64,128]{3,2,1,0:T(8,128)S(1)}, u32[]{:S(2)}, u32[]{:S(2)}) %collective-permute-start.27) | collective-permute-done | bytes 524320 | tf_op jit(solution)/shard_map/ppermute | solution.py:22
  115.3 1.6 collective-permute-start.34
  116.9 5.4 %collective-permute-start.22 = (f32[1,8,64,128]{3,2,1,0:T(8,128)S(1)}, f32[1,8,64,128]{3,2,1,0:T(8,128)S(1)}, u32[]{:S(2)}, u32[]{:S(2)}) collective-permute-start(f32[1,8,64,128]{3,2,1,0:T(8,128)S(1)} %get-tuple-element.210), channel_id=1, source_target_pairs={{0,80},{16,64},{32,112},{48,96},{64,16},{80,0},{96,48},{112,32},{1... | collective-permute-start | bytes 786440 | tf_op jit(solution)/shard_map/ppermute | solution.py:22
  125.5 11.6 %collective-permute-done.22.x = f32[1,8,64,128]{3,2,1,0:T(8,128)S(1)} collective-permute-done((f32[1,8,64,128]{3,2,1,0:T(8,128)S(1)}, f32[1,8,64,128]{3,2,1,0:T(8,128)S(1)}, u32[]{:S(2)}, u32[]{:S(2)}) %collective-permute-start.22) | collective-permute-done | bytes 262176 | tf_op jit(solution)/shard_map/ppermute | solution.py:22
  140.6 5.8 %collective-permute-done.32.other = f32[2,8,64,128]{3,2,1,0:T(8,128)S(1)} collective-permute-done((f32[2,8,64,128]{3,2,1,0:T(8,128)S(1)}, f32[2,8,64,128]{3,2,1,0:T(8,128)S(1)}, u32[]{:S(2)}, u32[]{:S(2)}) %collective-permute-start.32) | collective-permute-done | bytes 524320 | tf_op jit(solution)/shard_map/ppermute | solution.py:22
  146.8 2.4 %collective-permute-start.39 = (f32[2,8,64,128]{3,2,1,0:T(8,128)S(1)}, f32[2,8,64,128]{3,2,1,0:T(8,128)S(1)}, u32[]{:S(2)}, u32[]{:S(2)}) collective-permute-start(f32[2,8,64,128]{3,2,1,0:T(8,128)S(1)} %get-tuple-element.251.own), channel_id=1, source_target_pairs={{0,4},{1,5},{2,6},{3,7},{4,0},{5,1},{6,2},{7,3},{8,12},{9,13},{10,... | collective-permute-start | bytes 1572872 | tf_op jit(solution)/shard_map/ppermute | solution.py:22
  150.5 9.3 %collective-permute-done.31.other = f32[2,8,64,128]{3,2,1,0:T(8,128)S(1)} collective-permute-done((f32[2,8,64,128]{3,2,1,0:T(8,128)S(1)}, f32[2,8,64,128]{3,2,1,0:T(8,128)S(1)}, u32[]{:S(2)}, u32[]{:S(2)}) %collective-permute-start.31) | collective-permute-done | bytes 524320 | tf_op jit(solution)/shard_map/ppermute | solution.py:22
  160.2 1.6 collective-permute-start.38
  163.5 11.0 %collective-permute-done.40.other = f32[1,8,64,128]{3,2,1,0:T(8,128)S(1)} collective-permute-done((f32[1,8,64,128]{3,2,1,0:T(8,128)S(1)}, f32[1,8,64,128]{3,2,1,0:T(8,128)S(1)}, u32[]{:S(2)}, u32[]{:S(2)}) %collective-permute-start.40) | collective-permute-done | bytes 262176 | tf_op jit(solution)/shard_map/ppermute | solution.py:22
  175.8 3.3 %collective-permute-start.43 = (f32[1,8,64,128]{3,2,1,0:T(8,128)S(1)}, f32[1,8,64,128]{3,2,1,0:T(8,128)S(1)}, u32[]{:S(2)}, u32[]{:S(2)}) collective-permute-start(f32[1,8,64,128]{3,2,1,0:T(8,128)S(1)} %get-tuple-element.260.own), channel_id=1, source_target_pairs={{0,4},{1,5},{2,6},{3,7},{4,0},{5,1},{6,2},{7,3},{8,12},{9,13},{10,... | collective-permute-start | bytes 786440 | tf_op jit(solution)/shard_map/ppermute | solution.py:22
  180.7 2.0 collective-permute-start.41
  182.7 5.2 %collective-permute-done.43.other = f32[1,8,64,128]{3,2,1,0:T(8,128)S(1)} collective-permute-done((f32[1,8,64,128]{3,2,1,0:T(8,128)S(1)}, f32[1,8,64,128]{3,2,1,0:T(8,128)S(1)}, u32[]{:S(2)}, u32[]{:S(2)}) %collective-permute-start.43) | collective-permute-done | bytes 262176 | tf_op jit(solution)/shard_map/ppermute | solution.py:22
  188.2 1.6 collective-permute-start.45
  192.5 1.6 collective-permute-start.44
  196.2 4.1 %collective-permute-done.44.other = f32[1,8,64,128]{3,2,1,0:T(8,128)S(1)} collective-permute-done((f32[1,8,64,128]{3,2,1,0:T(8,128)S(1)}, f32[1,8,64,128]{3,2,1,0:T(8,128)S(1)}, u32[]{:S(2)}, u32[]{:S(2)}) %collective-permute-start.44) | collective-permute-done | bytes 262176 | tf_op jit(solution)/shard_map/ppermute | solution.py:22
  (114 shorter events, 41.8 us)
Async XLA Ops:
  0.0 0.7 copy-start
  2.3 11.2 %collective-permute-start.3 = (f32[2,8,64,128]{3,2,1,0:T(8,128)S(1)}, f32[2,8,64,128]{3,2,1,0:T(8,128)S(1)}, u32[]{:S(2)}, u32[]{:S(2)}) collective-permute-start(f32[2,8,64,128]{3,2,1,0:T(8,128)S(1)} %get-tuple-element.144.own), channel_id=1, source_target_pairs={{0,1},{1,0},{2,3},{3,2},{4,5},{5,4},{6,7},{7,6},{8,9},{9,8},{10,11... | collective-permute-start | bytes 1572872 | tf_op jit(solution)/shard_map/ppermute | solution.py:22
  2.4 3.2 %copy-start.1 = (s32[16]{0:T(128)S(1)}, s32[16]{0:T(128)}, u32[]{:S(2)}) copy-start(s32[16]{0:T(128)} %owner_map.17) | copy-start | bytes 196
  3.4 15.6 %collective-permute-start.2 = (f32[2,8,64,128]{3,2,1,0:T(8,128)S(1)}, f32[2,8,64,128]{3,2,1,0:T(8,128)S(1)}, u32[]{:S(2)}, u32[]{:S(2)}) collective-permute-start(f32[2,8,64,128]{3,2,1,0:T(8,128)S(1)} %get-tuple-element.143), channel_id=1, source_target_pairs={{0,2},{1,3},{2,0},{3,1},{4,6},{5,7},{6,4},{7,5},{8,10},{9,11},{10,... | collective-permute-start | bytes 1572872 | tf_op jit(solution)/shard_map/ppermute | solution.py:22
  7.1 14.2 %collective-permute-start.1 = (f32[2,8,64,128]{3,2,1,0:T(8,128)S(1)}, f32[2,8,64,128]{3,2,1,0:T(8,128)S(1)}, u32[]{:S(2)}, u32[]{:S(2)}) collective-permute-start(f32[2,8,64,128]{3,2,1,0:T(8,128)S(1)} %get-tuple-element.142), channel_id=1, source_target_pairs={{0,32},{16,48},{32,0},{48,16},{64,96},{80,112},{96,64},{112,80},{1... | collective-permute-start | bytes 1572872 | tf_op jit(solution)/shard_map/ppermute | solution.py:22
  10.4 15.7 %collective-permute-start = (f32[2,8,64,128]{3,2,1,0:T(8,128)S(1)}, f32[2,8,64,128]{3,2,1,0:T(8,128)S(1)}, u32[]{:S(2)}, u32[]{:S(2)}) collective-permute-start(f32[2,8,64,128]{3,2,1,0:T(8,128)S(1)} %get-tuple-element.141), channel_id=1, source_target_pairs={{0,16},{16,0},{32,48},{48,32},{64,80},{80,64},{96,112},{112,96},{1... | collective-permute-start | bytes 1572872 | tf_op jit(solution)/shard_map/ppermute | solution.py:22
  15.0 19.0 %collective-permute-start.6 = (f32[2,8,64,128]{3,2,1,0:T(8,128)S(1)}, f32[2,8,64,128]{3,2,1,0:T(8,128)S(1)}, u32[]{:S(2)}, u32[]{:S(2)}) collective-permute-start(f32[2,8,64,128]{3,2,1,0:T(8,128)S(1)} %get-tuple-element.161.own), channel_id=1, source_target_pairs={{0,2},{1,3},{2,0},{3,1},{4,6},{5,7},{6,4},{7,5},{8,10},{9,11},{10,... | collective-permute-start | bytes 1572872 | tf_op jit(solution)/shard_map/ppermute | solution.py:22
  16.8 18.0 %collective-permute-start.5 = (f32[2,8,64,128]{3,2,1,0:T(8,128)S(1)}, f32[2,8,64,128]{3,2,1,0:T(8,128)S(1)}, u32[]{:S(2)}, u32[]{:S(2)}) collective-permute-start(f32[2,8,64,128]{3,2,1,0:T(8,128)S(1)} %get-tuple-element.158), channel_id=1, source_target_pairs={{0,96},{16,112},{32,64},{48,80},{64,32},{80,48},{96,0},{112,16},{1... | collective-permute-start | bytes 1572872 | tf_op jit(solution)/shard_map/ppermute | solution.py:22
  21.3 16.4 %collective-permute-start.4 = (f32[2,8,64,128]{3,2,1,0:T(8,128)S(1)}, f32[2,8,64,128]{3,2,1,0:T(8,128)S(1)}, u32[]{:S(2)}, u32[]{:S(2)}) collective-permute-start(f32[2,8,64,128]{3,2,1,0:T(8,128)S(1)} %get-tuple-element.157.own), channel_id=1, source_target_pairs={{0,1},{1,0},{2,3},{3,2},{4,5},{5,4},{6,7},{7,6},{8,9},{9,8},{10,11... | collective-permute-start | bytes 1572872 | tf_op jit(solution)/shard_map/ppermute | solution.py:22
  22.4 18.1 %collective-permute-start.7 = (f32[2,8,64,128]{3,2,1,0:T(8,128)S(1)}, f32[2,8,64,128]{3,2,1,0:T(8,128)S(1)}, u32[]{:S(2)}, u32[]{:S(2)}) collective-permute-start(f32[2,8,64,128]{3,2,1,0:T(8,128)S(1)} %get-tuple-element.167), channel_id=1, source_target_pairs={{0,2},{1,3},{2,0},{3,1},{4,6},{5,7},{6,4},{7,5},{8,10},{9,11},{10,... | collective-permute-start | bytes 1572872 | tf_op jit(solution)/shard_map/ppermute | solution.py:22
  26.0 20.1 %collective-permute-start.12 = (f32[2,8,64,128]{3,2,1,0:T(8,128)S(1)}, f32[2,8,64,128]{3,2,1,0:T(8,128)S(1)}, u32[]{:S(2)}, u32[]{:S(2)}) collective-permute-start(f32[2,8,64,128]{3,2,1,0:T(8,128)S(1)} %get-tuple-element.175), channel_id=1, source_target_pairs={{0,48},{16,32},{32,16},{48,0},{64,112},{80,96},{96,80},{112,64},{1... | collective-permute-start | bytes 1572872 | tf_op jit(solution)/shard_map/ppermute | solution.py:22
  34.0 15.5 %collective-permute-start.11 = (f32[2,8,64,128]{3,2,1,0:T(8,128)S(1)}, f32[2,8,64,128]{3,2,1,0:T(8,128)S(1)}, u32[]{:S(2)}, u32[]{:S(2)}) collective-permute-start(f32[2,8,64,128]{3,2,1,0:T(8,128)S(1)} %get-tuple-element.174.own), channel_id=1, source_target_pairs={{0,1},{1,0},{2,3},{3,2},{4,5},{5,4},{6,7},{7,6},{8,9},{9,8},{10,11... | collective-permute-start | bytes 1572872 | tf_op jit(solution)/shard_map/ppermute | solution.py:22
  34.8 15.6 %collective-permute-start.10 = (f32[2,8,64,128]{3,2,1,0:T(8,128)S(1)}, f32[2,8,64,128]{3,2,1,0:T(8,128)S(1)}, u32[]{:S(2)}, u32[]{:S(2)}) collective-permute-start(f32[2,8,64,128]{3,2,1,0:T(8,128)S(1)} %get-tuple-element.173), channel_id=1, source_target_pairs={{0,6},{1,7},{2,4},{3,5},{4,2},{5,3},{6,0},{7,1},{8,14},{9,15},{10,... | collective-permute-start | bytes 1572872 | tf_op jit(solution)/shard_map/ppermute | solution.py:22
  37.7 13.8 %collective-permute-start.9 = (f32[2,8,64,128]{3,2,1,0:T(8,128)S(1)}, f32[2,8,64,128]{3,2,1,0:T(8,128)S(1)}, u32[]{:S(2)}, u32[]{:S(2)}) collective-permute-start(f32[2,8,64,128]{3,2,1,0:T(8,128)S(1)} %get-tuple-element.171.own), channel_id=1, source_target_pairs={{0,1},{1,0},{2,3},{3,2},{4,5},{5,4},{6,7},{7,6},{8,9},{9,8},{10,11... | collective-permute-start | bytes 1572872 | tf_op jit(solution)/shard_map/ppermute | solution.py:22
  40.6 14.5 %collective-permute-start.13 = (f32[2,8,64,128]{3,2,1,0:T(8,128)S(1)}, f32[2,8,64,128]{3,2,1,0:T(8,128)S(1)}, u32[]{:S(2)}, u32[]{:S(2)}) collective-permute-start(f32[2,8,64,128]{3,2,1,0:T(8,128)S(1)} %get-tuple-element.182.own), channel_id=1, source_target_pairs={{0,2},{1,3},{2,0},{3,1},{4,6},{5,7},{6,4},{7,5},{8,10},{9,11},{10,... | collective-permute-start | bytes 1572872 | tf_op jit(solution)/shard_map/ppermute | solution.py:22
  46.2 14.8 %collective-permute-start.8 = (f32[2,8,64,128]{3,2,1,0:T(8,128)S(1)}, f32[2,8,64,128]{3,2,1,0:T(8,128)S(1)}, u32[]{:S(2)}, u32[]{:S(2)}) collective-permute-start(f32[2,8,64,128]{3,2,1,0:T(8,128)S(1)} %get-tuple-element.170), channel_id=1, source_target_pairs={{0,64},{16,80},{32,96},{48,112},{64,0},{80,16},{96,32},{112,48},{1... | collective-permute-start | bytes 1572872 | tf_op jit(solution)/shard_map/ppermute | solution.py:22
  49.5 11.9 %collective-permute-start.16 = (f32[2,8,64,128]{3,2,1,0:T(8,128)S(1)}, f32[2,8,64,128]{3,2,1,0:T(8,128)S(1)}, u32[]{:S(2)}, u32[]{:S(2)}) collective-permute-start(f32[2,8,64,128]{3,2,1,0:T(8,128)S(1)} %get-tuple-element.188.own), channel_id=1, source_target_pairs={{0,1},{1,0},{2,3},{3,2},{4,5},{5,4},{6,7},{7,6},{8,9},{9,8},{10,11... | collective-permute-start | bytes 1572872 | tf_op jit(solution)/shard_map/ppermute | solution.py:22
  50.4 15.9 %collective-permute-start.19 = (f32[2,8,64,128]{3,2,1,0:T(8,128)S(1)}, f32[2,8,64,128]{3,2,1,0:T(8,128)S(1)}, u32[]{:S(2)}, u32[]{:S(2)}) collective-permute-start(f32[2,8,64,128]{3,2,1,0:T(8,128)S(1)} %get-tuple-element.194.own), channel_id=1, source_target_pairs={{0,2},{1,3},{2,0},{3,1},{4,6},{5,7},{6,4},{7,5},{8,10},{9,11},{10,... | collective-permute-start | bytes 1572872 | tf_op jit(solution)/shard_map/ppermute | solution.py:22
  51.4 21.1 %collective-permute-start.18 = (f32[2,8,64,128]{3,2,1,0:T(8,128)S(1)}, f32[2,8,64,128]{3,2,1,0:T(8,128)S(1)}, u32[]{:S(2)}, u32[]{:S(2)}) collective-permute-start(f32[2,8,64,128]{3,2,1,0:T(8,128)S(1)} %get-tuple-element.193.own), channel_id=1, source_target_pairs={{0,8},{1,9},{2,10},{3,11},{4,12},{5,13},{6,14},{7,15},{8,0},{9,1},... | collective-permute-start | bytes 1572872 | tf_op jit(solution)/shard_map/ppermute | solution.py:22
  55.8 21.8 %collective-permute-start.17 = (f32[2,8,64,128]{3,2,1,0:T(8,128)S(1)}, f32[2,8,64,128]{3,2,1,0:T(8,128)S(1)}, u32[]{:S(2)}, u32[]{:S(2)}) collective-permute-start(f32[2,8,64,128]{3,2,1,0:T(8,128)S(1)} %get-tuple-element.192), channel_id=1, source_target_pairs={{0,6},{1,7},{2,4},{3,5},{4,2},{5,3},{6,0},{7,1},{8,14},{9,15},{10,... | collective-permute-start | bytes 1572872 | tf_op jit(solution)/shard_map/ppermute | solution.py:22
  61.0 19.2 %collective-permute-start.15 = (f32[2,8,64,128]{3,2,1,0:T(8,128)S(1)}, f32[2,8,64,128]{3,2,1,0:T(8,128)S(1)}, u32[]{:S(2)}, u32[]{:S(2)}) collective-permute-start(f32[2,8,64,128]{3,2,1,0:T(8,128)S(1)} %get-tuple-element.187.own), channel_id=1, source_target_pairs={{0,2},{1,3},{2,0},{3,1},{4,6},{5,7},{6,4},{7,5},{8,10},{9,11},{10,... | collective-permute-start | bytes 1572872 | tf_op jit(solution)/shard_map/ppermute | solution.py:22
  61.4 22.6 %collective-permute-start.14 = (f32[2,8,64,128]{3,2,1,0:T(8,128)S(1)}, f32[2,8,64,128]{3,2,1,0:T(8,128)S(1)}, u32[]{:S(2)}, u32[]{:S(2)}) collective-permute-start(f32[2,8,64,128]{3,2,1,0:T(8,128)S(1)} %get-tuple-element.186.own), channel_id=1, source_target_pairs={{0,1},{1,0},{2,3},{3,2},{4,5},{5,4},{6,7},{7,6},{8,9},{9,8},{10,11... | collective-permute-start | bytes 1572872 | tf_op jit(solution)/shard_map/ppermute | solution.py:22
  66.3 19.9 %collective-permute-start.21 = (f32[2,8,64,128]{3,2,1,0:T(8,128)S(1)}, f32[2,8,64,128]{3,2,1,0:T(8,128)S(1)}, u32[]{:S(2)}, u32[]{:S(2)}) collective-permute-start(f32[2,8,64,128]{3,2,1,0:T(8,128)S(1)} %get-tuple-element.205), channel_id=1, source_target_pairs={{0,112},{16,96},{32,80},{48,64},{64,48},{80,32},{96,16},{112,0},{1... | collective-permute-start | bytes 1572872 | tf_op jit(solution)/shard_map/ppermute | solution.py:22
  72.5 19.9 %collective-permute-start.20 = (f32[2,8,64,128]{3,2,1,0:T(8,128)S(1)}, f32[2,8,64,128]{3,2,1,0:T(8,128)S(1)}, u32[]{:S(2)}, u32[]{:S(2)}) collective-permute-start(f32[2,8,64,128]{3,2,1,0:T(8,128)S(1)} %get-tuple-element.204.own), channel_id=1, source_target_pairs={{0,4},{1,5},{2,6},{3,7},{4,0},{5,1},{6,2},{7,3},{8,12},{9,13},{10,... | collective-permute-start | bytes 1572872 | tf_op jit(solution)/shard_map/ppermute | solution.py:22
  78.0 22.6 %collective-permute-start.25 = (f32[2,8,64,128]{3,2,1,0:T(8,128)S(1)}, f32[2,8,64,128]{3,2,1,0:T(8,128)S(1)}, u32[]{:S(2)}, u32[]{:S(2)}) collective-permute-start(f32[2,8,64,128]{3,2,1,0:T(8,128)S(1)} %get-tuple-element.213.own), channel_id=1, source_target_pairs={{0,8},{1,9},{2,10},{3,11},{4,12},{5,13},{6,14},{7,15},{8,0},{9,1},... | collective-permute-start | bytes 1572872 | tf_op jit(solution)/shard_map/ppermute | solution.py:22
  80.2 18.9 %collective-permute-start.29 = (f32[1,8,64,128]{3,2,1,0:T(8,128)S(1)}, f32[1,8,64,128]{3,2,1,0:T(8,128)S(1)}, u32[]{:S(2)}, u32[]{:S(2)}) collective-permute-start(f32[1,8,64,128]{3,2,1,0:T(8,128)S(1)} %get-tuple-element.220), channel_id=1, source_target_pairs={{0,80},{16,64},{32,112},{48,96},{64,16},{80,0},{96,48},{112,32},{1... | collective-permute-start | bytes 786440 | tf_op jit(solution)/shard_map/ppermute | solution.py:22
  83.9 20.9 %collective-permute-start.28 = (f32[2,8,64,128]{3,2,1,0:T(8,128)S(1)}, f32[2,8,64,128]{3,2,1,0:T(8,128)S(1)}, u32[]{:S(2)}, u32[]{:S(2)}) collective-permute-start(f32[2,8,64,128]{3,2,1,0:T(8,128)S(1)} %get-tuple-element.219.own), channel_id=1, source_target_pairs={{0,2},{1,3},{2,0},{3,1},{4,6},{5,7},{6,4},{7,5},{8,10},{9,11},{10,... | collective-permute-start | bytes 1572872 | tf_op jit(solution)/shard_map/ppermute | solution.py:22
  86.2 28.7 %collective-permute-start.27 = (f32[2,8,64,128]{3,2,1,0:T(8,128)S(1)}, f32[2,8,64,128]{3,2,1,0:T(8,128)S(1)}, u32[]{:S(2)}, u32[]{:S(2)}) collective-permute-start(f32[2,8,64,128]{3,2,1,0:T(8,128)S(1)} %get-tuple-element.218.own), channel_id=1, source_target_pairs={{0,4},{1,5},{2,6},{3,7},{4,0},{5,1},{6,2},{7,3},{8,12},{9,13},{10,... | collective-permute-start | bytes 1572872 | tf_op jit(solution)/shard_map/ppermute | solution.py:22
  92.4 24.5 %collective-permute-start.26 = (f32[2,8,64,128]{3,2,1,0:T(8,128)S(1)}, f32[2,8,64,128]{3,2,1,0:T(8,128)S(1)}, u32[]{:S(2)}, u32[]{:S(2)}) collective-permute-start(f32[2,8,64,128]{3,2,1,0:T(8,128)S(1)} %get-tuple-element.217.own), channel_id=1, source_target_pairs={{0,1},{1,0},{2,3},{3,2},{4,5},{5,4},{6,7},{7,6},{8,9},{9,8},{10,11... | collective-permute-start | bytes 1572872 | tf_op jit(solution)/shard_map/ppermute | solution.py:22
  99.1 23.6 %collective-permute-start.24 = (f32[2,8,64,128]{3,2,1,0:T(8,128)S(1)}, f32[2,8,64,128]{3,2,1,0:T(8,128)S(1)}, u32[]{:S(2)}, u32[]{:S(2)}) collective-permute-start(f32[2,8,64,128]{3,2,1,0:T(8,128)S(1)} %get-tuple-element.212.own), channel_id=1, source_target_pairs={{0,8},{1,9},{2,10},{3,11},{4,12},{5,13},{6,14},{7,15},{8,0},{9,1},... | collective-permute-start | bytes 1572872 | tf_op jit(solution)/shard_map/ppermute | solution.py:22
  100.6 23.3 %collective-permute-start.23 = (f32[2,8,64,128]{3,2,1,0:T(8,128)S(1)}, f32[2,8,64,128]{3,2,1,0:T(8,128)S(1)}, u32[]{:S(2)}, u32[]{:S(2)}) collective-permute-start(f32[2,8,64,128]{3,2,1,0:T(8,128)S(1)} %get-tuple-element.211.own), channel_id=1, source_target_pairs={{0,2},{1,3},{2,0},{3,1},{4,6},{5,7},{6,4},{7,5},{8,10},{9,11},{10,... | collective-permute-start | bytes 1572872 | tf_op jit(solution)/shard_map/ppermute | solution.py:22
  105.3 32.2 %collective-permute-start.35 = (f32[2,8,64,128]{3,2,1,0:T(8,128)S(1)}, f32[2,8,64,128]{3,2,1,0:T(8,128)S(1)}, u32[]{:S(2)}, u32[]{:S(2)}) collective-permute-start(f32[2,8,64,128]{3,2,1,0:T(8,128)S(1)} %get-tuple-element.236.own), channel_id=1, source_target_pairs={{0,4},{1,5},{2,6},{3,7},{4,0},{5,1},{6,2},{7,3},{8,12},{9,13},{10,... | collective-permute-start | bytes 1572872 | tf_op jit(solution)/shard_map/ppermute | solution.py:22
  115.3 24.0 %collective-permute-start.34 = (f32[2,8,64,128]{3,2,1,0:T(8,128)S(1)}, f32[2,8,64,128]{3,2,1,0:T(8,128)S(1)}, u32[]{:S(2)}, u32[]{:S(2)}) collective-permute-start(f32[2,8,64,128]{3,2,1,0:T(8,128)S(1)} %get-tuple-element.234.own), channel_id=1, source_target_pairs={{0,8},{1,9},{2,10},{3,11},{4,12},{5,13},{6,14},{7,15},{8,0},{9,1},... | collective-permute-start | bytes 1572872 | tf_op jit(solution)/shard_map/ppermute | solution.py:22
  116.9 20.3 %collective-permute-start.22 = (f32[1,8,64,128]{3,2,1,0:T(8,128)S(1)}, f32[1,8,64,128]{3,2,1,0:T(8,128)S(1)}, u32[]{:S(2)}, u32[]{:S(2)}) collective-permute-start(f32[1,8,64,128]{3,2,1,0:T(8,128)S(1)} %get-tuple-element.210), channel_id=1, source_target_pairs={{0,80},{16,64},{32,112},{48,96},{64,16},{80,0},{96,48},{112,32},{1... | collective-permute-start | bytes 786440 | tf_op jit(solution)/shard_map/ppermute | solution.py:22
  122.7 23.7 %collective-permute-start.32 = (f32[2,8,64,128]{3,2,1,0:T(8,128)S(1)}, f32[2,8,64,128]{3,2,1,0:T(8,128)S(1)}, u32[]{:S(2)}, u32[]{:S(2)}) collective-permute-start(f32[2,8,64,128]{3,2,1,0:T(8,128)S(1)} %get-tuple-element.230.own), channel_id=1, source_target_pairs={{0,2},{1,3},{2,0},{3,1},{4,6},{5,7},{6,4},{7,5},{8,10},{9,11},{10,... | collective-permute-start | bytes 1572872 | tf_op jit(solution)/shard_map/ppermute | solution.py:22
  123.9 13.3 %collective-permute-start.33 = (f32[1,8,64,128]{3,2,1,0:T(8,128)S(1)}, f32[1,8,64,128]{3,2,1,0:T(8,128)S(1)}, u32[]{:S(2)}, u32[]{:S(2)}) collective-permute-start(f32[1,8,64,128]{3,2,1,0:T(8,128)S(1)} %get-tuple-element.231.own), channel_id=1, source_target_pairs={{0,1},{1,0},{2,3},{3,2},{4,5},{5,4},{6,7},{7,6},{8,9},{9,8},{10,11... | collective-permute-start | bytes 786440 | tf_op jit(solution)/shard_map/ppermute | solution.py:22
  137.2 22.6 %collective-permute-start.31 = (f32[2,8,64,128]{3,2,1,0:T(8,128)S(1)}, f32[2,8,64,128]{3,2,1,0:T(8,128)S(1)}, u32[]{:S(2)}, u32[]{:S(2)}) collective-permute-start(f32[2,8,64,128]{3,2,1,0:T(8,128)S(1)} %get-tuple-element.229.own), channel_id=1, source_target_pairs={{0,4},{1,5},{2,6},{3,7},{4,0},{5,1},{6,2},{7,3},{8,12},{9,13},{10,... | collective-permute-start | bytes 1572872 | tf_op jit(solution)/shard_map/ppermute | solution.py:22
  137.9 24.2 %collective-permute-start.36 = (f32[2,8,64,128]{3,2,1,0:T(8,128)S(1)}, f32[2,8,64,128]{3,2,1,0:T(8,128)S(1)}, u32[]{:S(2)}, u32[]{:S(2)}) collective-permute-start(f32[2,8,64,128]{3,2,1,0:T(8,128)S(1)} %get-tuple-element.244.own), channel_id=1, source_target_pairs={{0,8},{1,9},{2,10},{3,11},{4,12},{5,13},{6,14},{7,15},{8,0},{9,1},... | collective-permute-start | bytes 1572872 | tf_op jit(solution)/shard_map/ppermute | solution.py:22
  146.8 28.0 %collective-permute-start.39 = (f32[2,8,64,128]{3,2,1,0:T(8,128)S(1)}, f32[2,8,64,128]{3,2,1,0:T(8,128)S(1)}, u32[]{:S(2)}, u32[]{:S(2)}) collective-permute-start(f32[2,8,64,128]{3,2,1,0:T(8,128)S(1)} %get-tuple-element.251.own), channel_id=1, source_target_pairs={{0,4},{1,5},{2,6},{3,7},{4,0},{5,1},{6,2},{7,3},{8,12},{9,13},{10,... | collective-permute-start | bytes 1572872 | tf_op jit(solution)/shard_map/ppermute | solution.py:22
  149.1 12.7 %collective-permute-start.30 = (f32[1,8,64,128]{3,2,1,0:T(8,128)S(1)}, f32[1,8,64,128]{3,2,1,0:T(8,128)S(1)}, u32[]{:S(2)}, u32[]{:S(2)}) collective-permute-start(f32[1,8,64,128]{3,2,1,0:T(8,128)S(1)} %get-tuple-element.228.own), channel_id=1, source_target_pairs={{0,1},{1,0},{2,3},{3,2},{4,5},{5,4},{6,7},{7,6},{8,9},{9,8},{10,11... | collective-permute-start | bytes 786440 | tf_op jit(solution)/shard_map/ppermute | solution.py:22
  149.1 25.3 %collective-permute-start.40 = (f32[1,8,64,128]{3,2,1,0:T(8,128)S(1)}, f32[1,8,64,128]{3,2,1,0:T(8,128)S(1)}, u32[]{:S(2)}, u32[]{:S(2)}) collective-permute-start(f32[1,8,64,128]{3,2,1,0:T(8,128)S(1)} %get-tuple-element.252.own), channel_id=1, source_target_pairs={{0,2},{1,3},{2,0},{3,1},{4,6},{5,7},{6,4},{7,5},{8,10},{9,11},{10,... | collective-permute-start | bytes 786440 | tf_op jit(solution)/shard_map/ppermute | solution.py:22
  160.2 18.9 %collective-permute-start.38 = (f32[2,8,64,128]{3,2,1,0:T(8,128)S(1)}, f32[2,8,64,128]{3,2,1,0:T(8,128)S(1)}, u32[]{:S(2)}, u32[]{:S(2)}) collective-permute-start(f32[2,8,64,128]{3,2,1,0:T(8,128)S(1)} %get-tuple-element.249.own), channel_id=1, source_target_pairs={{0,8},{1,9},{2,10},{3,11},{4,12},{5,13},{6,14},{7,15},{8,0},{9,1},... | collective-permute-start | bytes 1572872 | tf_op jit(solution)/shard_map/ppermute | solution.py:22
  163.4 17.0 %collective-permute-start.37 = (f32[1,8,64,128]{3,2,1,0:T(8,128)S(1)}, f32[1,8,64,128]{3,2,1,0:T(8,128)S(1)}, u32[]{:S(2)}, u32[]{:S(2)}) collective-permute-start(f32[1,8,64,128]{3,2,1,0:T(8,128)S(1)} %get-tuple-element.248.own), channel_id=1, source_target_pairs={{0,2},{1,3},{2,0},{3,1},{4,6},{5,7},{6,4},{7,5},{8,10},{9,11},{10,... | collective-permute-start | bytes 786440 | tf_op jit(solution)/shard_map/ppermute | solution.py:22
  175.2 14.6 %collective-permute-start.42 = (f32[2,8,64,128]{3,2,1,0:T(8,128)S(1)}, f32[2,8,64,128]{3,2,1,0:T(8,128)S(1)}, u32[]{:S(2)}, u32[]{:S(2)}) collective-permute-start(f32[2,8,64,128]{3,2,1,0:T(8,128)S(1)} %get-tuple-element.258.own), channel_id=1, source_target_pairs={{0,8},{1,9},{2,10},{3,11},{4,12},{5,13},{6,14},{7,15},{8,0},{9,1},... | collective-permute-start | bytes 1572872 | tf_op jit(solution)/shard_map/ppermute | solution.py:22
  175.8 12.1 %collective-permute-start.43 = (f32[1,8,64,128]{3,2,1,0:T(8,128)S(1)}, f32[1,8,64,128]{3,2,1,0:T(8,128)S(1)}, u32[]{:S(2)}, u32[]{:S(2)}) collective-permute-start(f32[1,8,64,128]{3,2,1,0:T(8,128)S(1)} %get-tuple-element.260.own), channel_id=1, source_target_pairs={{0,4},{1,5},{2,6},{3,7},{4,0},{5,1},{6,2},{7,3},{8,12},{9,13},{10,... | collective-permute-start | bytes 786440 | tf_op jit(solution)/shard_map/ppermute | solution.py:22
  180.7 11.5 %collective-permute-start.41 = (f32[1,8,64,128]{3,2,1,0:T(8,128)S(1)}, f32[1,8,64,128]{3,2,1,0:T(8,128)S(1)}, u32[]{:S(2)}, u32[]{:S(2)}) collective-permute-start(f32[1,8,64,128]{3,2,1,0:T(8,128)S(1)} %get-tuple-element.257.own), channel_id=1, source_target_pairs={{0,4},{1,5},{2,6},{3,7},{4,0},{5,1},{6,2},{7,3},{8,12},{9,13},{10,... | collective-permute-start | bytes 786440 | tf_op jit(solution)/shard_map/ppermute | solution.py:22
  188.2 7.0 %collective-permute-start.45 = (f32[1,8,64,128]{3,2,1,0:T(8,128)S(1)}, f32[1,8,64,128]{3,2,1,0:T(8,128)S(1)}, u32[]{:S(2)}, u32[]{:S(2)}) collective-permute-start(f32[1,8,64,128]{3,2,1,0:T(8,128)S(1)} %get-tuple-element.265.own), channel_id=1, source_target_pairs={{0,8},{1,9},{2,10},{3,11},{4,12},{5,13},{6,14},{7,15},{8,0},{9,1},... | collective-permute-start | bytes 786440 | tf_op jit(solution)/shard_map/ppermute | solution.py:22
  192.5 7.7 %collective-permute-start.44 = (f32[1,8,64,128]{3,2,1,0:T(8,128)S(1)}, f32[1,8,64,128]{3,2,1,0:T(8,128)S(1)}, u32[]{:S(2)}, u32[]{:S(2)}) collective-permute-start(f32[1,8,64,128]{3,2,1,0:T(8,128)S(1)} %get-tuple-element.264.own), channel_id=1, source_target_pairs={{0,8},{1,9},{2,10},{3,11},{4,12},{5,13},{6,14},{7,15},{8,0},{9,1},... | collective-permute-start | bytes 786440 | tf_op jit(solution)/shard_map/ppermute | solution.py:22
where the time goes:
time: 202 us; the launch traced here: 201 us
  starting transfers between devices  77.8 us (39%)
  waiting for transfers between devices  74.2 us (37%)
  Pallas kernels  48 us (24%)
    ppermute x46, starting transfers between devices, permute_xor(): lax.ppermute(x, axis, [(i, i ^ mask) for i in range(lax.axis_size(axis))])  77.8 us
    ppermute x46, waiting for transfers between devices, permute_xor(): lax.ppermute(x, axis, [(i, i ^ mask) for i in range(lax.axis_size(axis))])  74.2 us
    pallas_call x66, Pallas kernels, call(): pl.pallas_call(body, in_specs=in_specs + [ANY] * len(tokens), out_specs=o...  48 us
  transfers between devices with their start and end apart: 46, of which 17 were waited for; matrix products, arithmetic and copies ran while one was open for 0% of the time, Pallas kernels for 23%

commit v1 on v0

--- a/solution.py
+++ b/solution.py
@@ -254,14 +254,14 @@
 ORDER = (0, 2, 1, 6, 3, 4, 7, 5)
 CUTS = {5: (2, 2)}
 
-PICK, LAND, SEND, FETCH, LEND = range(5)
+PICK, ADMIT, LEND, BORROW, FETCH = range(-5, 0)
 PLAN = (
-    (PICK, 0), (LEND, 0), (PICK, 1), (PICK, 2), LAND, (SEND, 0), (PICK, 3), LAND, (FETCH, 1), LAND, (LEND, 1),
-    (PICK, 4), LAND, (FETCH, 0), (FETCH, 3), LAND, LAND, LAND, (SEND, 1), (FETCH, 2), LAND, (PICK, 5), LAND,
-    LAND, (SEND, 2), LAND, LAND, LAND, (SEND, 3), LAND, LAND, (PICK, 6), LAND, LAND, LAND, (PICK, 7),
-    (SEND, 4), LAND, LAND, LAND, LAND, (SEND, 5), (PICK, 8), LAND, LAND, LAND, LAND, LAND, (SEND, 6), LAND,
-    LAND, LAND, LAND, LAND, LAND, (SEND, 7), LAND, LAND, LAND, LAND, (SEND, 8), LAND, LAND, LAND, LAND, LAND,
-    LAND, LAND, LAND, LAND,
+    (LEND, 0), (PICK, 1), (LEND, 1), (PICK, 0), (PICK, 3), (PICK, 4), (LEND, 2), (PICK, 2), (BORROW, 0),
+    (FETCH, 0), (ADMIT, 1), (0, 0), (PICK, 5), (BORROW, 1), (FETCH, 1), (ADMIT, 3), (0, 1), (1, 0),
+    (ADMIT, 4), (ADMIT, 2), (FETCH, 3), (0, 3), (FETCH, 2), (BORROW, 2), (PICK, 6), (PICK, 8), (1, 1),
+    (ADMIT, 5), (2, 0), (0, 4), (1, 3), (0, 2), (3, 0), (1, 4), (2, 1), (ADMIT, 6), (0, 5), (1, 2), (PICK, 7),
+    (ADMIT, 8), (2, 3), (0, 6), (0, 8), (1, 5), (2, 2), (ADMIT, 7), (3, 1), (2, 4), (3, 3), (1, 6), (3, 2),
+    (2, 5), (1, 8), (0, 7), (3, 4), (2, 6), (1, 7), (2, 8), (3, 5), (2, 7), (3, 6), (3, 8), (3, 7),
 )
 
 
@@ -295,85 +295,70 @@
     chunks = chunks_of(parts, local_slots, groups)
     state, other, fetched, lent = {}, {}, {}, {}
     token, coeffs = None, None
-    flying = collections.deque()
-
-    def exchange(i, level):
-        other[i] = permute_xor(state[i], "blk", 1 << (level % bit_count))
-        flying.append((level, i))
+
+    def start(i, mask):
+        other[i] = permute_xor(state[i], "blk", mask)
+
+    def mask_of(level):
+        return 1 << (level % bit_count)
+
+    def pick(i):
+        nonlocal token
+        chunk = chunks[i]
+        state[i], token = pick_slots(
+            place, owner_map, rows, [chunk], local_slots, block_cols, token
+        )
+        if chunk.part:
+            state[i] = permute_xor(state[i], "ma", chunk.part)
+        else:
+            start(i, mask_of(0))
+
+    def admit(i):
+        nonlocal token
+        state[i], token = gate(state[i], token)
+        start(i, mask_of(0))
+
+    def lend(i):
+        nonlocal token
+        lent[i], token = pick_factors(place, factors, 1, chunks[i], parts, token)
+        lent[i] = permute_xor(lent[i], "blk", mask_of(1))
+
+    def borrow(i):
+        nonlocal token
+        lent[i], token = gate(lent[i], token)
 
     def fetch(level):
         nonlocal token
-        if level not in fetched:
-            fetched[level], token = fetch_factors(factors, level, token)
-        return fetched[level]
-
-    def pick(i):
-        nonlocal token
-        state[i], token = pick_slots(
-            place, owner_map, rows, [chunks[i]], local_slots, block_cols, token
-        )
-        if chunks[i].part:
-            state[i] = permute_xor(state[i], "ma", chunks[i].part)
-            flying.append((-1, i))
+        fetched[level], token = fetch_factors(factors, level, token)
+
+    def product(level, i):
+        nonlocal token, coeffs
+        if level == level_count - 1:
+            coeffs, token = last_product(
+                place, fetched[level], state[i], other[i], chunks[i], parts, token, coeffs
+            )
+        elif level == 1 and i in lent:
+            state[i], theirs, token = both_products(
+                place, fetched[1], lent.pop(i), state[i], other[i], chunks[i], parts, token
+            )
+            other[i] = permute_xor(theirs, "blk", mask_of(1) ^ mask_of(2))
         else:
-            exchange(i, 0)
-
-    def lend(i):
-        nonlocal token
-        lent[i], token = pick_factors(place, factors, 1, chunks[i], parts, token)
-        lent[i] = permute_xor(lent[i], "blk", 1 << (1 % bit_count))
-        flying.append((-2, i))
-
-    def land(level, i):
-        nonlocal token, coeffs
-        if level == -2:
-            lent[i], token = gate(lent[i], token)
-            return
-        if level == 1 and i in lent:
-            state[i], theirs, token = both_products(
-                place, fetch(1), lent.pop(i), state[i], other[i], chunks[i], parts, token
-            )
-            bits = (1 << (1 % bit_count)) ^ (1 << (2 % bit_count))
-            other[i] = permute_xor(theirs, "blk", bits)
-            flying.append((2, i))
-            return
-        if level < 0:
-            state[i], token = gate(state[i], token)
-        elif level == 0 and not chunks[i].part:
-            state[i], token = early_product(
-                place, factors, state[i], other[i], chunks[i], parts, token
-            )
-        elif level < level_count - 1:
-            state[i], token = level_product(
-                place, fetch(level), state[i], other[i], chunks[i], parts, token
-            )
+            if level == 0 and not chunks[i].part:
+                state[i], token = early_product(
+                    place, factors, state[i], other[i], chunks[i], parts, token
+                )
+            else:
+                state[i], token = level_product(
+                    place, fetched[level], state[i], other[i], chunks[i], parts, token
+                )
+            start(i, mask_of(level + 1))
+
+    steps = {PICK: pick, ADMIT: admit, LEND: lend, BORROW: borrow, FETCH: fetch}
+    for what, i in PLAN:
+        if what in steps:
+            steps[what](i)
         else:
-            coeffs, token = last_product(
-                place, fetch(level), state[i], other[i], chunks[i], parts, token, coeffs
-            )
-            return
-        if level == 0:
-            ready.append(i)
-        else:
-            exchange(i, level + 1)
-
-    def send(i):
-        nonlocal token
-        if ready[-1] != i or not fresh:
-            state[i], token = gate(state[i], token)
-        ready.remove(i)
-        exchange(i, 1)
-
-    ready, fresh = [], False
-    for step in PLAN:
-        if step == LAND:
-            level, i = flying.popleft()
-            land(level, i)
-            fresh = level == 0
-        else:
-            what, i = step
-            {PICK: pick, SEND: send, FETCH: fetch, LEND: lend}[what](i)
-            fresh = False
+            product(what, i)
     return coeffs
 
 

time: 202 us -> 198 us (0.980)
  starting transfers between devices: 77.8 us -> 70.9 us
  waiting for transfers between devices: 74.2 us -> 76.7 us
    ppermute x46 -> x47, starting transfers between devices: 77.8 us -> 70.9 us  [permute_xor(): lax.ppermute(x, axis, [(i, i ^ mask) for i in range(lax.axis_size(axis))])]
    ppermute x46 -> x47, waiting for transfers between devices: 74.2 us -> 76.7 us  [permute_xor(): lax.ppermute(x, axis, [(i, i ^ mask) for i in range(lax.axis_size(axis))])]
    pallas_call x66 -> x63, Pallas kernels: 48 us -> 49.3 us  [call(): pl.pallas_call(body, in_specs=in_specs + [ANY] * len(tokens), out_specs=o...]
  transfers between devices with their start and end apart: 46 -> 47, of which waited for: 17 -> 22; matrix products, arithmetic and copies ran while one was open for 0% -> 0% of each run, Pallas kernels for 23% -> 24%
where the time goes in v1:
time: 198 us
  waiting for transfers between devices  76.7 us (39%)
  starting transfers between devices  70.9 us (36%)
  Pallas kernels  49.3 us (25%)
    ppermute x47, waiting for transfers between devices, permute_xor(): lax.ppermute(x, axis, [(i, i ^ mask) for i in range(lax.axis_size(axis))])  76.7 us
    ppermute x47, starting transfers between devices, permute_xor(): lax.ppermute(x, axis, [(i, i ^ mask) for i in range(lax.axis_size(axis))])  70.9 us
    pallas_call x63, Pallas kernels, call(): pl.pallas_call(body, in_specs=in_specs + [ANY] * len(tokens), out_specs=o...  49.3 us
  transfers between devices with their start and end apart: 47, of which 22 were waited for; matrix products, arithmetic and copies ran while one was open for 0% of the time, Pallas kernels for 24%

profile of v1, /device:TPU:0, one launch (start us, length us, event | category | flops | bytes accessed | tf_op | source)
XLA Modules:
  0.0 197.7 jit_solution(14461698895618524141)
XLA Ops:
  1.1 2.1 %collective-permute-start.5 = (f32[2,8,64,128]{3,2,1,0:T(8,128)S(1)}, f32[2,8,64,128]{3,2,1,0:T(8,128)S(1)}, u32[]{:S(2)}, u32[]{:S(2)}) collective-permute-start(f32[2,8,64,128]{3,2,1,0:T(8,128)S(1)} %get-tuple-element.145), channel_id=1, source_target_pairs={{0,2},{1,3},{2,0},{3,1},{4,6},{5,7},{6,4},{7,5},{8,10},{9,11},{10,... | collective-permute-start | bytes 1572872 | tf_op jit(solution)/shard_map/ppermute | solution.py:22
  3.2 1.6 pick_slots.9
  4.8 1.7 collective-permute-start.4
  7.5 1.6 pick_slots.10
  9.4 1.6 pick_slots.11
  11.0 2.3 %collective-permute-start.8 = (f32[2,8,64,128]{3,2,1,0:T(8,128)S(1)}, f32[2,8,64,128]{3,2,1,0:T(8,128)S(1)}, u32[]{:S(2)}, u32[]{:S(2)}) collective-permute-start(f32[2,8,64,128]{3,2,1,0:T(8,128)S(1)} %get-tuple-element.158), channel_id=1, source_target_pairs={{0,96},{16,112},{32,64},{48,80},{64,32},{80,48},{96,0},{112,16},{1... | collective-permute-start | bytes 1572872 | tf_op jit(solution)/shard_map/ppermute | solution.py:22
  13.2 1.6 pick_slots.12
  15.9 1.6 pick_slots.13
  17.5 2.2 %fetch_factors.4 = (f32[2,64,64,128]{3,2,1,0:T(8,128)S(1)}, f32[8,128]{1,0:T(8,128)S(1)}) custom-call(f32[4,2,64,64,128]{4,3,2,1,0:T(8,128)} %factors.15, f32[8,128]{1,0:T(8,128)S(1)} %get-tuple-element.147.refs_0_), custom_call_target="tpu_custom_call" | custom-call | tf_op jit(solution)/shard_map/fetch_factors/pallas_call | solution.py:35
  21.4 2.0 %collective-permute-start.6 = (f32[2,8,64,128]{3,2,1,0:T(8,128)S(1)}, f32[2,8,64,128]{3,2,1,0:T(8,128)S(1)}, u32[]{:S(2)}, u32[]{:S(2)}) collective-permute-start(f32[2,8,64,128]{3,2,1,0:T(8,128)S(1)} %get-tuple-element.155.own), channel_id=1, source_target_pairs={{0,2},{1,3},{2,0},{3,1},{4,6},{5,7},{6,4},{7,5},{8,10},{9,11},{10,... | collective-permute-start | bytes 1572872 | tf_op jit(solution)/shard_map/ppermute | solution.py:22
  23.4 3.1 %collective-permute-start.1 = (f32[2,8,64,128]{3,2,1,0:T(8,128)S(1)}, f32[2,8,64,128]{3,2,1,0:T(8,128)S(1)}, u32[]{:S(2)}, u32[]{:S(2)}) collective-permute-start(f32[2,8,64,128]{3,2,1,0:T(8,128)S(1)} %get-tuple-element.141), channel_id=1, source_target_pairs={{0,48},{16,32},{32,16},{48,0},{64,112},{80,96},{96,80},{112,64},{1... | collective-permute-start | bytes 1572872 | tf_op jit(solution)/shard_map/ppermute | solution.py:22
  27.2 3.1 %collective-permute-start = (f32[2,8,64,128]{3,2,1,0:T(8,128)S(1)}, f32[2,8,64,128]{3,2,1,0:T(8,128)S(1)}, u32[]{:S(2)}, u32[]{:S(2)}) collective-permute-start(f32[2,8,64,128]{3,2,1,0:T(8,128)S(1)} %get-tuple-element.140), channel_id=1, source_target_pairs={{0,16},{16,0},{32,48},{48,32},{64,80},{80,64},{96,112},{112,96},{1... | collective-permute-start | bytes 1572872 | tf_op jit(solution)/shard_map/ppermute | solution.py:22
  30.3 1.6 pick_slots.14
  31.9 2.2 %fetch_factors.5 = (f32[2,64,64,128]{3,2,1,0:T(8,128)S(1)}, f32[8,128]{1,0:T(8,128)S(1)}) custom-call(f32[4,2,64,64,128]{4,3,2,1,0:T(8,128)} %factors.15, f32[8,128]{1,0:T(8,128)S(1)} %get-tuple-element.152.refs_0_), custom_call_target="tpu_custom_call" | custom-call | tf_op jit(solution)/shard_map/fetch_factors/pallas_call | solution.py:35
  34.3 2.0 %collective-permute-start.10 = (f32[2,8,64,128]{3,2,1,0:T(8,128)S(1)}, f32[2,8,64,128]{3,2,1,0:T(8,128)S(1)}, u32[]{:S(2)}, u32[]{:S(2)}) collective-permute-start(f32[2,8,64,128]{3,2,1,0:T(8,128)S(1)} %get-tuple-element.170), channel_id=1, source_target_pairs={{0,2},{1,3},{2,0},{3,1},{4,6},{5,7},{6,4},{7,5},{8,10},{9,11},{10,... | collective-permute-start | bytes 1572872 | tf_op jit(solution)/shard_map/ppermute | solution.py:22
  37.5 1.7 collective-permute-start.16
  40.5 2.7 %collective-permute-start.15 = (f32[2,8,64,128]{3,2,1,0:T(8,128)S(1)}, f32[2,8,64,128]{3,2,1,0:T(8,128)S(1)}, u32[]{:S(2)}, u32[]{:S(2)}) collective-permute-start(f32[2,8,64,128]{3,2,1,0:T(8,128)S(1)} %get-tuple-element.178), channel_id=1, source_target_pairs={{0,64},{16,80},{32,96},{48,112},{64,0},{80,16},{96,32},{112,48},{1... | collective-permute-start | bytes 1572872 | tf_op jit(solution)/shard_map/ppermute | solution.py:22
  43.3 7.0 %collective-permute-done.x = f32[2,8,64,128]{3,2,1,0:T(8,128)S(1)} collective-permute-done((f32[2,8,64,128]{3,2,1,0:T(8,128)S(1)}, f32[2,8,64,128]{3,2,1,0:T(8,128)S(1)}, u32[]{:S(2)}, u32[]{:S(2)}) %collective-permute-start) | collective-permute-done | bytes 524320 | tf_op jit(solution)/shard_map/ppermute | solution.py:22
  50.3 2.5 %collective-permute-start.14 = (f32[2,8,64,128]{3,2,1,0:T(8,128)S(1)}, f32[2,8,64,128]{3,2,1,0:T(8,128)S(1)}, u32[]{:S(2)}, u32[]{:S(2)}) collective-permute-start(f32[2,8,64,128]{3,2,1,0:T(8,128)S(1)} %get-tuple-element.177), channel_id=1, source_target_pairs={{0,6},{1,7},{2,4},{3,5},{4,2},{5,3},{6,0},{7,1},{8,14},{9,15},{10,... | collective-permute-start | bytes 1572872 | tf_op jit(solution)/shard_map/ppermute | solution.py:22
  52.8 2.2 %fetch_factors.6 = (f32[2,64,64,128]{3,2,1,0:T(8,128)S(1)}, f32[8,128]{1,0:T(8,128)S(1)}) custom-call(f32[4,2,64,64,128]{4,3,2,1,0:T(8,128)} %factors.15, f32[8,128]{1,0:T(8,128)S(1)} %get-tuple-element.164.refs_0_), custom_call_target="tpu_custom_call" | custom-call | tf_op jit(solution)/shard_map/fetch_factors/pallas_call | solution.py:35
  56.6 2.2 %fetch_factors.7 = (f32[2,64,64,128]{3,2,1,0:T(8,128)S(1)}, f32[8,128]{1,0:T(8,128)S(1)}) custom-call(f32[4,2,64,64,128]{4,3,2,1,0:T(8,128)} %factors.15, f32[8,128]{1,0:T(8,128)S(1)} %get-tuple-element.168.refs_0_), custom_call_target="tpu_custom_call" | custom-call | tf_op jit(solution)/shard_map/fetch_factors/pallas_call | solution.py:35
  58.8 1.6 pick_slots.15
  63.0 1.7 collective-permute-done.14.other
  65.1 1.6 collective-permute-start.22
  67.8 2.4 %collective-permute-start.20 = (f32[2,8,64,128]{3,2,1,0:T(8,128)S(1)}, f32[2,8,64,128]{3,2,1,0:T(8,128)S(1)}, u32[]{:S(2)}, u32[]{:S(2)}) collective-permute-start(f32[2,8,64,128]{3,2,1,0:T(8,128)S(1)} %get-tuple-element.193), channel_id=1, source_target_pairs={{0,6},{1,7},{2,4},{3,5},{4,2},{5,3},{6,0},{7,1},{8,14},{9,15},{10,... | collective-permute-start | bytes 1572872 | tf_op jit(solution)/shard_map/ppermute | solution.py:22
  71.5 6.2 %collective-permute-start.19 = (f32[2,8,64,128]{3,2,1,0:T(8,128)S(1)}, f32[2,8,64,128]{3,2,1,0:T(8,128)S(1)}, u32[]{:S(2)}, u32[]{:S(2)}) collective-permute-start(f32[2,8,64,128]{3,2,1,0:T(8,128)S(1)} %get-tuple-element.191), channel_id=1, source_target_pairs={{0,112},{16,96},{32,80},{48,64},{64,48},{80,32},{96,16},{112,0},{1... | collective-permute-start | bytes 1572872 | tf_op jit(solution)/shard_map/ppermute | solution.py:22
  78.6 2.0 %collective-permute-start.17 = (f32[2,8,64,128]{3,2,1,0:T(8,128)S(1)}, f32[2,8,64,128]{3,2,1,0:T(8,128)S(1)}, u32[]{:S(2)}, u32[]{:S(2)}) collective-permute-start(f32[2,8,64,128]{3,2,1,0:T(8,128)S(1)} %get-tuple-element.189.own), channel_id=1, source_target_pairs={{0,2},{1,3},{2,0},{3,1},{4,6},{5,7},{6,4},{7,5},{8,10},{9,11},{10,... | collective-permute-start | bytes 1572872 | tf_op jit(solution)/shard_map/ppermute | solution.py:22
  82.8 3.9 %collective-permute-start.29 = (f32[2,8,64,128]{3,2,1,0:T(8,128)S(1)}, f32[2,8,64,128]{3,2,1,0:T(8,128)S(1)}, u32[]{:S(2)}, u32[]{:S(2)}) collective-permute-start(f32[2,8,64,128]{3,2,1,0:T(8,128)S(1)} %get-tuple-element.211.own), channel_id=1, source_target_pairs={{0,4},{1,5},{2,6},{3,7},{4,0},{5,1},{6,2},{7,3},{8,12},{9,13},{10,... | collective-permute-start | bytes 1572872 | tf_op jit(solution)/shard_map/ppermute | solution.py:22
  87.6 4.9 %collective-permute-done.19.x = f32[2,8,64,128]{3,2,1,0:T(8,128)S(1)} collective-permute-done((f32[2,8,64,128]{3,2,1,0:T(8,128)S(1)}, f32[2,8,64,128]{3,2,1,0:T(8,128)S(1)}, u32[]{:S(2)}, u32[]{:S(2)}) %collective-permute-start.19) | collective-permute-done | bytes 524320 | tf_op jit(solution)/shard_map/ppermute | solution.py:22
  92.4 1.7 collective-permute-start.26
  96.4 2.5 %collective-permute-start.24 = (f32[2,8,64,128]{3,2,1,0:T(8,128)S(1)}, f32[2,8,64,128]{3,2,1,0:T(8,128)S(1)}, u32[]{:S(2)}, u32[]{:S(2)}) collective-permute-start(f32[2,8,64,128]{3,2,1,0:T(8,128)S(1)} %get-tuple-element.205), channel_id=1, source_target_pairs={{0,6},{1,7},{2,4},{3,5},{4,2},{5,3},{6,0},{7,1},{8,14},{9,15},{10,... | collective-permute-start | bytes 1572872 | tf_op jit(solution)/shard_map/ppermute | solution.py:22
  100.4 4.7 %collective-permute-done.26.x = f32[1,8,64,128]{3,2,1,0:T(8,128)S(1)} collective-permute-done((f32[1,8,64,128]{3,2,1,0:T(8,128)S(1)}, f32[1,8,64,128]{3,2,1,0:T(8,128)S(1)}, u32[]{:S(2)}, u32[]{:S(2)}) %collective-permute-start.26) | collective-permute-done | bytes 262176 | tf_op jit(solution)/shard_map/ppermute | solution.py:22
  105.1 3.7 %collective-permute-done.29.other = f32[2,8,64,128]{3,2,1,0:T(8,128)S(1)} collective-permute-done((f32[2,8,64,128]{3,2,1,0:T(8,128)S(1)}, f32[2,8,64,128]{3,2,1,0:T(8,128)S(1)}, u32[]{:S(2)}, u32[]{:S(2)}) %collective-permute-start.29) | collective-permute-done | bytes 524320 | tf_op jit(solution)/shard_map/ppermute | solution.py:22
  108.8 1.8 collective-permute-start.35
  110.6 5.7 %collective-permute-start.23 = (f32[1,8,64,128]{3,2,1,0:T(8,128)S(1)}, f32[1,8,64,128]{3,2,1,0:T(8,128)S(1)}, u32[]{:S(2)}, u32[]{:S(2)}) collective-permute-start(f32[1,8,64,128]{3,2,1,0:T(8,128)S(1)} %get-tuple-element.203), channel_id=1, source_target_pairs={{0,80},{16,64},{32,112},{48,96},{64,16},{80,0},{96,48},{112,32},{1... | collective-permute-start | bytes 786440 | tf_op jit(solution)/shard_map/ppermute | solution.py:22
  121.2 13.5 %collective-permute-done.23.x = f32[1,8,64,128]{3,2,1,0:T(8,128)S(1)} collective-permute-done((f32[1,8,64,128]{3,2,1,0:T(8,128)S(1)}, f32[1,8,64,128]{3,2,1,0:T(8,128)S(1)}, u32[]{:S(2)}, u32[]{:S(2)}) %collective-permute-start.23) | collective-permute-done | bytes 262176 | tf_op jit(solution)/shard_map/ppermute | solution.py:22
  136.8 3.7 %collective-permute-done.34.other = f32[2,8,64,128]{3,2,1,0:T(8,128)S(1)} collective-permute-done((f32[2,8,64,128]{3,2,1,0:T(8,128)S(1)}, f32[2,8,64,128]{3,2,1,0:T(8,128)S(1)}, u32[]{:S(2)}, u32[]{:S(2)}) %collective-permute-start.34) | collective-permute-done | bytes 524320 | tf_op jit(solution)/shard_map/ppermute | solution.py:22
  141.8 1.9 collective-permute-start.40
  144.1 7.7 %collective-permute-done.33.other = f32[2,8,64,128]{3,2,1,0:T(8,128)S(1)} collective-permute-done((f32[2,8,64,128]{3,2,1,0:T(8,128)S(1)}, f32[2,8,64,128]{3,2,1,0:T(8,128)S(1)}, u32[]{:S(2)}, u32[]{:S(2)}) %collective-permute-start.33) | collective-permute-done | bytes 524320 | tf_op jit(solution)/shard_map/ppermute | solution.py:22
  153.1 3.0 %collective-permute-done.32.other = f32[2,8,64,128]{3,2,1,0:T(8,128)S(1)} collective-permute-done((f32[2,8,64,128]{3,2,1,0:T(8,128)S(1)}, f32[2,8,64,128]{3,2,1,0:T(8,128)S(1)}, u32[]{:S(2)}, u32[]{:S(2)}) %collective-permute-start.32) | collective-permute-done | bytes 524320 | tf_op jit(solution)/shard_map/ppermute | solution.py:22
  156.5 1.7 collective-permute-done.31.other
  158.8 2.1 %collective-permute-start.38 = (f32[1,8,64,128]{3,2,1,0:T(8,128)S(1)}, f32[1,8,64,128]{3,2,1,0:T(8,128)S(1)}, u32[]{:S(2)}, u32[]{:S(2)}) collective-permute-start(f32[1,8,64,128]{3,2,1,0:T(8,128)S(1)} %get-tuple-element.237.own), channel_id=1, source_target_pairs={{0,2},{1,3},{2,0},{3,1},{4,6},{5,7},{6,4},{7,5},{8,10},{9,11},{10,... | collective-permute-start | bytes 786440 | tf_op jit(solution)/shard_map/ppermute | solution.py:22
  161.1 3.5 %collective-permute-start.43 = (f32[1,8,64,128]{3,2,1,0:T(8,128)S(1)}, f32[1,8,64,128]{3,2,1,0:T(8,128)S(1)}, u32[]{:S(2)}, u32[]{:S(2)}) collective-permute-start(f32[1,8,64,128]{3,2,1,0:T(8,128)S(1)} %get-tuple-element.247.own), channel_id=1, source_target_pairs={{0,4},{1,5},{2,6},{3,7},{4,0},{5,1},{6,2},{7,3},{8,12},{9,13},{10,... | collective-permute-start | bytes 786440 | tf_op jit(solution)/shard_map/ppermute | solution.py:22
  165.9 7.1 %collective-permute-done.39.other = f32[2,8,64,128]{3,2,1,0:T(8,128)S(1)} collective-permute-done((f32[2,8,64,128]{3,2,1,0:T(8,128)S(1)}, f32[2,8,64,128]{3,2,1,0:T(8,128)S(1)}, u32[]{:S(2)}, u32[]{:S(2)}) %collective-permute-start.39) | collective-permute-done | bytes 524320 | tf_op jit(solution)/shard_map/ppermute | solution.py:22
  175.4 4.0 %collective-permute-start.41 = (f32[1,8,64,128]{3,2,1,0:T(8,128)S(1)}, f32[1,8,64,128]{3,2,1,0:T(8,128)S(1)}, u32[]{:S(2)}, u32[]{:S(2)}) collective-permute-start(f32[1,8,64,128]{3,2,1,0:T(8,128)S(1)} %get-tuple-element.244.own), channel_id=1, source_target_pairs={{0,4},{1,5},{2,6},{3,7},{4,0},{5,1},{6,2},{7,3},{8,12},{9,13},{10,... | collective-permute-start | bytes 786440 | tf_op jit(solution)/shard_map/ppermute | solution.py:22
  179.3 4.8 %collective-permute-done.43.other = f32[1,8,64,128]{3,2,1,0:T(8,128)S(1)} collective-permute-done((f32[1,8,64,128]{3,2,1,0:T(8,128)S(1)}, f32[1,8,64,128]{3,2,1,0:T(8,128)S(1)}, u32[]{:S(2)}, u32[]{:S(2)}) %collective-permute-start.43) | collective-permute-done | bytes 262176 | tf_op jit(solution)/shard_map/ppermute | solution.py:22
  190.0 3.6 %collective-permute-done.45.other = f32[1,8,64,128]{3,2,1,0:T(8,128)S(1)} collective-permute-done((f32[1,8,64,128]{3,2,1,0:T(8,128)S(1)}, f32[1,8,64,128]{3,2,1,0:T(8,128)S(1)}, u32[]{:S(2)}, u32[]{:S(2)}) %collective-permute-start.45) | collective-permute-done | bytes 262176 | tf_op jit(solution)/shard_map/ppermute | solution.py:22
  194.6 1.9 collective-permute-done.44.other
  (111 shorter events, 45.4 us)
Async XLA Ops:
  0.0 3.2 %copy-start = (s32[16]{0:T(128)S(1)}, s32[16]{0:T(128)}, u32[]{:S(2)}) copy-start(s32[16]{0:T(128)} %owner_map.17) | copy-start | bytes 196
  1.1 16.4 %collective-permute-start.5 = (f32[2,8,64,128]{3,2,1,0:T(8,128)S(1)}, f32[2,8,64,128]{3,2,1,0:T(8,128)S(1)}, u32[]{:S(2)}, u32[]{:S(2)}) collective-permute-start(f32[2,8,64,128]{3,2,1,0:T(8,128)S(1)} %get-tuple-element.145), channel_id=1, source_target_pairs={{0,2},{1,3},{2,0},{3,1},{4,6},{5,7},{6,4},{7,5},{8,10},{9,11},{10,... | collective-permute-start | bytes 1572872 | tf_op jit(solution)/shard_map/ppermute | solution.py:22
  4.8 15.0 %collective-permute-start.4 = (f32[2,8,64,128]{3,2,1,0:T(8,128)S(1)}, f32[2,8,64,128]{3,2,1,0:T(8,128)S(1)}, u32[]{:S(2)}, u32[]{:S(2)}) collective-permute-start(f32[2,8,64,128]{3,2,1,0:T(8,128)S(1)} %get-tuple-element.144), channel_id=1, source_target_pairs={{0,32},{16,48},{32,0},{48,16},{64,96},{80,112},{96,64},{112,80},{1... | collective-permute-start | bytes 1572872 | tf_op jit(solution)/shard_map/ppermute | solution.py:22
  9.1 10.8 %collective-permute-start.3 = (f32[2,8,64,128]{3,2,1,0:T(8,128)S(1)}, f32[2,8,64,128]{3,2,1,0:T(8,128)S(1)}, u32[]{:S(2)}, u32[]{:S(2)}) collective-permute-start(f32[2,8,64,128]{3,2,1,0:T(8,128)S(1)} %get-tuple-element.143.own), channel_id=1, source_target_pairs={{0,1},{1,0},{2,3},{3,2},{4,5},{5,4},{6,7},{7,6},{8,9},{9,8},{10,11... | collective-permute-start | bytes 1572872 | tf_op jit(solution)/shard_map/ppermute | solution.py:22
  9.2 18.0 %collective-permute-start.2 = (f32[2,8,64,128]{3,2,1,0:T(8,128)S(1)}, f32[2,8,64,128]{3,2,1,0:T(8,128)S(1)}, u32[]{:S(2)}, u32[]{:S(2)}) collective-permute-start(f32[2,8,64,128]{3,2,1,0:T(8,128)S(1)} %get-tuple-element.142), channel_id=1, source_target_pairs={{0,2},{1,3},{2,0},{3,1},{4,6},{5,7},{6,4},{7,5},{8,10},{9,11},{10,... | collective-permute-start | bytes 1572872 | tf_op jit(solution)/shard_map/ppermute | solution.py:22
  11.0 23.2 %collective-permute-start.8 = (f32[2,8,64,128]{3,2,1,0:T(8,128)S(1)}, f32[2,8,64,128]{3,2,1,0:T(8,128)S(1)}, u32[]{:S(2)}, u32[]{:S(2)}) collective-permute-start(f32[2,8,64,128]{3,2,1,0:T(8,128)S(1)} %get-tuple-element.158), channel_id=1, source_target_pairs={{0,96},{16,112},{32,64},{48,80},{64,32},{80,48},{96,0},{112,16},{1... | collective-permute-start | bytes 1572872 | tf_op jit(solution)/shard_map/ppermute | solution.py:22
  19.8 14.5 %collective-permute-start.7 = (f32[2,8,64,128]{3,2,1,0:T(8,128)S(1)}, f32[2,8,64,128]{3,2,1,0:T(8,128)S(1)}, u32[]{:S(2)}, u32[]{:S(2)}) collective-permute-start(f32[2,8,64,128]{3,2,1,0:T(8,128)S(1)} %get-tuple-element.157.own), channel_id=1, source_target_pairs={{0,1},{1,0},{2,3},{3,2},{4,5},{5,4},{6,7},{7,6},{8,9},{9,8},{10,11... | collective-permute-start | bytes 1572872 | tf_op jit(solution)/shard_map/ppermute | solution.py:22
  21.4 16.2 %collective-permute-start.6 = (f32[2,8,64,128]{3,2,1,0:T(8,128)S(1)}, f32[2,8,64,128]{3,2,1,0:T(8,128)S(1)}, u32[]{:S(2)}, u32[]{:S(2)}) collective-permute-start(f32[2,8,64,128]{3,2,1,0:T(8,128)S(1)} %get-tuple-element.155.own), channel_id=1, source_target_pairs={{0,2},{1,3},{2,0},{3,1},{4,6},{5,7},{6,4},{7,5},{8,10},{9,11},{10,... | collective-permute-start | bytes 1572872 | tf_op jit(solution)/shard_map/ppermute | solution.py:22
  23.4 17.2 %collective-permute-start.1 = (f32[2,8,64,128]{3,2,1,0:T(8,128)S(1)}, f32[2,8,64,128]{3,2,1,0:T(8,128)S(1)}, u32[]{:S(2)}, u32[]{:S(2)}) collective-permute-start(f32[2,8,64,128]{3,2,1,0:T(8,128)S(1)} %get-tuple-element.141), channel_id=1, source_target_pairs={{0,48},{16,32},{32,16},{48,0},{64,112},{80,96},{96,80},{112,64},{1... | collective-permute-start | bytes 1572872 | tf_op jit(solution)/shard_map/ppermute | solution.py:22
  27.2 23.1 %collective-permute-start = (f32[2,8,64,128]{3,2,1,0:T(8,128)S(1)}, f32[2,8,64,128]{3,2,1,0:T(8,128)S(1)}, u32[]{:S(2)}, u32[]{:S(2)}) collective-permute-start(f32[2,8,64,128]{3,2,1,0:T(8,128)S(1)} %get-tuple-element.140), channel_id=1, source_target_pairs={{0,16},{16,0},{32,48},{48,32},{64,80},{80,64},{96,112},{112,96},{1... | collective-permute-start | bytes 1572872 | tf_op jit(solution)/shard_map/ppermute | solution.py:22
  34.2 18.6 %collective-permute-start.9 = (f32[2,8,64,128]{3,2,1,0:T(8,128)S(1)}, f32[2,8,64,128]{3,2,1,0:T(8,128)S(1)}, u32[]{:S(2)}, u32[]{:S(2)}) collective-permute-start(f32[2,8,64,128]{3,2,1,0:T(8,128)S(1)} %get-tuple-element.166.own), channel_id=1, source_target_pairs={{0,1},{1,0},{2,3},{3,2},{4,5},{5,4},{6,7},{7,6},{8,9},{9,8},{10,11... | collective-permute-start | bytes 1572872 | tf_op jit(solution)/shard_map/ppermute | solution.py:22
  34.3 21.2 %collective-permute-start.10 = (f32[2,8,64,128]{3,2,1,0:T(8,128)S(1)}, f32[2,8,64,128]{3,2,1,0:T(8,128)S(1)}, u32[]{:S(2)}, u32[]{:S(2)}) collective-permute-start(f32[2,8,64,128]{3,2,1,0:T(8,128)S(1)} %get-tuple-element.170), channel_id=1, source_target_pairs={{0,2},{1,3},{2,0},{3,1},{4,6},{5,7},{6,4},{7,5},{8,10},{9,11},{10,... | collective-permute-start | bytes 1572872 | tf_op jit(solution)/shard_map/ppermute | solution.py:22
  37.5 24.4 %collective-permute-start.16 = (f32[2,8,64,128]{3,2,1,0:T(8,128)S(1)}, f32[2,8,64,128]{3,2,1,0:T(8,128)S(1)}, u32[]{:S(2)}, u32[]{:S(2)}) collective-permute-start(f32[2,8,64,128]{3,2,1,0:T(8,128)S(1)} %get-tuple-element.180.own), channel_id=1, source_target_pairs={{0,2},{1,3},{2,0},{3,1},{4,6},{5,7},{6,4},{7,5},{8,10},{9,11},{10,... | collective-permute-start | bytes 1572872 | tf_op jit(solution)/shard_map/ppermute | solution.py:22
  40.5 22.4 %collective-permute-start.15 = (f32[2,8,64,128]{3,2,1,0:T(8,128)S(1)}, f32[2,8,64,128]{3,2,1,0:T(8,128)S(1)}, u32[]{:S(2)}, u32[]{:S(2)}) collective-permute-start(f32[2,8,64,128]{3,2,1,0:T(8,128)S(1)} %get-tuple-element.178), channel_id=1, source_target_pairs={{0,64},{16,80},{32,96},{48,112},{64,0},{80,16},{96,32},{112,48},{1... | collective-permute-start | bytes 1572872 | tf_op jit(solution)/shard_map/ppermute | solution.py:22
  50.3 14.4 %collective-permute-start.14 = (f32[2,8,64,128]{3,2,1,0:T(8,128)S(1)}, f32[2,8,64,128]{3,2,1,0:T(8,128)S(1)}, u32[]{:S(2)}, u32[]{:S(2)}) collective-permute-start(f32[2,8,64,128]{3,2,1,0:T(8,128)S(1)} %get-tuple-element.177), channel_id=1, source_target_pairs={{0,6},{1,7},{2,4},{3,5},{4,2},{5,3},{6,0},{7,1},{8,14},{9,15},{10,... | collective-permute-start | bytes 1572872 | tf_op jit(solution)/shard_map/ppermute | solution.py:22
  52.8 13.9 %collective-permute-start.13 = (f32[2,8,64,128]{3,2,1,0:T(8,128)S(1)}, f32[2,8,64,128]{3,2,1,0:T(8,128)S(1)}, u32[]{:S(2)}, u32[]{:S(2)}) collective-permute-start(f32[2,8,64,128]{3,2,1,0:T(8,128)S(1)} %get-tuple-element.175.own), channel_id=1, source_target_pairs={{0,1},{1,0},{2,3},{3,2},{4,5},{5,4},{6,7},{7,6},{8,9},{9,8},{10,11... | collective-permute-start | bytes 1572872 | tf_op jit(solution)/shard_map/ppermute | solution.py:22
  55.5 16.0 %collective-permute-start.12 = (f32[2,8,64,128]{3,2,1,0:T(8,128)S(1)}, f32[2,8,64,128]{3,2,1,0:T(8,128)S(1)}, u32[]{:S(2)}, u32[]{:S(2)}) collective-permute-start(f32[2,8,64,128]{3,2,1,0:T(8,128)S(1)} %get-tuple-element.174.own), channel_id=1, source_target_pairs={{0,2},{1,3},{2,0},{3,1},{4,6},{5,7},{6,4},{7,5},{8,10},{9,11},{10,... | collective-permute-start | bytes 1572872 | tf_op jit(solution)/shard_map/ppermute | solution.py:22
  62.0 16.1 %collective-permute-start.11 = (f32[2,8,64,128]{3,2,1,0:T(8,128)S(1)}, f32[2,8,64,128]{3,2,1,0:T(8,128)S(1)}, u32[]{:S(2)}, u32[]{:S(2)}) collective-permute-start(f32[2,8,64,128]{3,2,1,0:T(8,128)S(1)} %get-tuple-element.173.own), channel_id=1, source_target_pairs={{0,1},{1,0},{2,3},{3,2},{4,5},{5,4},{6,7},{7,6},{8,9},{9,8},{10,11... | collective-permute-start | bytes 1572872 | tf_op jit(solution)/shard_map/ppermute | solution.py:22
  65.1 13.5 %collective-permute-start.22 = (f32[2,8,64,128]{3,2,1,0:T(8,128)S(1)}, f32[2,8,64,128]{3,2,1,0:T(8,128)S(1)}, u32[]{:S(2)}, u32[]{:S(2)}) collective-permute-start(f32[2,8,64,128]{3,2,1,0:T(8,128)S(1)} %get-tuple-element.195.own), channel_id=1, source_target_pairs={{0,8},{1,9},{2,10},{3,11},{4,12},{5,13},{6,14},{7,15},{8,0},{9,1},... | collective-permute-start | bytes 1572872 | tf_op jit(solution)/shard_map/ppermute | solution.py:22
  67.1 15.7 %collective-permute-start.21 = (f32[2,8,64,128]{3,2,1,0:T(8,128)S(1)}, f32[2,8,64,128]{3,2,1,0:T(8,128)S(1)}, u32[]{:S(2)}, u32[]{:S(2)}) collective-permute-start(f32[2,8,64,128]{3,2,1,0:T(8,128)S(1)} %get-tuple-element.194.own), channel_id=1, source_target_pairs={{0,2},{1,3},{2,0},{3,1},{4,6},{5,7},{6,4},{7,5},{8,10},{9,11},{10,... | collective-permute-start | bytes 1572872 | tf_op jit(solution)/shard_map/ppermute | solution.py:22
  67.8 19.3 %collective-permute-start.20 = (f32[2,8,64,128]{3,2,1,0:T(8,128)S(1)}, f32[2,8,64,128]{3,2,1,0:T(8,128)S(1)}, u32[]{:S(2)}, u32[]{:S(2)}) collective-permute-start(f32[2,8,64,128]{3,2,1,0:T(8,128)S(1)} %get-tuple-element.193), channel_id=1, source_target_pairs={{0,6},{1,7},{2,4},{3,5},{4,2},{5,3},{6,0},{7,1},{8,14},{9,15},{10,... | collective-permute-start | bytes 1572872 | tf_op jit(solution)/shard_map/ppermute | solution.py:22
  71.5 20.9 %collective-permute-start.19 = (f32[2,8,64,128]{3,2,1,0:T(8,128)S(1)}, f32[2,8,64,128]{3,2,1,0:T(8,128)S(1)}, u32[]{:S(2)}, u32[]{:S(2)}) collective-permute-start(f32[2,8,64,128]{3,2,1,0:T(8,128)S(1)} %get-tuple-element.191), channel_id=1, source_target_pairs={{0,112},{16,96},{32,80},{48,64},{64,48},{80,32},{96,16},{112,0},{1... | collective-permute-start | bytes 1572872 | tf_op jit(solution)/shard_map/ppermute | solution.py:22
  78.1 16.0 %collective-permute-start.18 = (f32[2,8,64,128]{3,2,1,0:T(8,128)S(1)}, f32[2,8,64,128]{3,2,1,0:T(8,128)S(1)}, u32[]{:S(2)}, u32[]{:S(2)}) collective-permute-start(f32[2,8,64,128]{3,2,1,0:T(8,128)S(1)} %get-tuple-element.190.own), channel_id=1, source_target_pairs={{0,1},{1,0},{2,3},{3,2},{4,5},{5,4},{6,7},{7,6},{8,9},{9,8},{10,11... | collective-permute-start | bytes 1572872 | tf_op jit(solution)/shard_map/ppermute | solution.py:22
  78.6 17.0 %collective-permute-start.17 = (f32[2,8,64,128]{3,2,1,0:T(8,128)S(1)}, f32[2,8,64,128]{3,2,1,0:T(8,128)S(1)}, u32[]{:S(2)}, u32[]{:S(2)}) collective-permute-start(f32[2,8,64,128]{3,2,1,0:T(8,128)S(1)} %get-tuple-element.189.own), channel_id=1, source_target_pairs={{0,2},{1,3},{2,0},{3,1},{4,6},{5,7},{6,4},{7,5},{8,10},{9,11},{10,... | collective-permute-start | bytes 1572872 | tf_op jit(solution)/shard_map/ppermute | solution.py:22
  82.8 26.0 %collective-permute-start.29 = (f32[2,8,64,128]{3,2,1,0:T(8,128)S(1)}, f32[2,8,64,128]{3,2,1,0:T(8,128)S(1)}, u32[]{:S(2)}, u32[]{:S(2)}) collective-permute-start(f32[2,8,64,128]{3,2,1,0:T(8,128)S(1)} %get-tuple-element.211.own), channel_id=1, source_target_pairs={{0,4},{1,5},{2,6},{3,7},{4,0},{5,1},{6,2},{7,3},{8,12},{9,13},{10,... | collective-permute-start | bytes 1572872 | tf_op jit(solution)/shard_map/ppermute | solution.py:22
  92.4 18.2 %collective-permute-start.28 = (f32[2,8,64,128]{3,2,1,0:T(8,128)S(1)}, f32[2,8,64,128]{3,2,1,0:T(8,128)S(1)}, u32[]{:S(2)}, u32[]{:S(2)}) collective-permute-start(f32[2,8,64,128]{3,2,1,0:T(8,128)S(1)} %get-tuple-element.210.own), channel_id=1, source_target_pairs={{0,1},{1,0},{2,3},{3,2},{4,5},{5,4},{6,7},{7,6},{8,9},{9,8},{10,11... | collective-permute-start | bytes 1572872 | tf_op jit(solution)/shard_map/ppermute | solution.py:22
  92.4 12.6 %collective-permute-start.26 = (f32[1,8,64,128]{3,2,1,0:T(8,128)S(1)}, f32[1,8,64,128]{3,2,1,0:T(8,128)S(1)}, u32[]{:S(2)}, u32[]{:S(2)}) collective-permute-start(f32[1,8,64,128]{3,2,1,0:T(8,128)S(1)} %get-tuple-element.207), channel_id=1, source_target_pairs={{0,80},{16,64},{32,112},{48,96},{64,16},{80,0},{96,48},{112,32},{1... | collective-permute-start | bytes 786440 | tf_op jit(solution)/shard_map/ppermute | solution.py:22
  94.6 23.0 %collective-permute-start.25 = (f32[2,8,64,128]{3,2,1,0:T(8,128)S(1)}, f32[2,8,64,128]{3,2,1,0:T(8,128)S(1)}, u32[]{:S(2)}, u32[]{:S(2)}) collective-permute-start(f32[2,8,64,128]{3,2,1,0:T(8,128)S(1)} %get-tuple-element.206.own), channel_id=1, source_target_pairs={{0,2},{1,3},{2,0},{3,1},{4,6},{5,7},{6,4},{7,5},{8,10},{9,11},{10,... | collective-permute-start | bytes 1572872 | tf_op jit(solution)/shard_map/ppermute | solution.py:22
  96.4 23.6 %collective-permute-start.24 = (f32[2,8,64,128]{3,2,1,0:T(8,128)S(1)}, f32[2,8,64,128]{3,2,1,0:T(8,128)S(1)}, u32[]{:S(2)}, u32[]{:S(2)}) collective-permute-start(f32[2,8,64,128]{3,2,1,0:T(8,128)S(1)} %get-tuple-element.205), channel_id=1, source_target_pairs={{0,6},{1,7},{2,4},{3,5},{4,2},{5,3},{6,0},{7,1},{8,14},{9,15},{10,... | collective-permute-start | bytes 1572872 | tf_op jit(solution)/shard_map/ppermute | solution.py:22
  105.1 12.1 %collective-permute-start.27 = (f32[1,8,64,128]{3,2,1,0:T(8,128)S(1)}, f32[1,8,64,128]{3,2,1,0:T(8,128)S(1)}, u32[]{:S(2)}, u32[]{:S(2)}) collective-permute-start(f32[1,8,64,128]{3,2,1,0:T(8,128)S(1)} %get-tuple-element.209.own), channel_id=1, source_target_pairs={{0,1},{1,0},{2,3},{3,2},{4,5},{5,4},{6,7},{7,6},{8,9},{9,8},{10,11... | collective-permute-start | bytes 786440 | tf_op jit(solution)/shard_map/ppermute | solution.py:22
  108.8 26.2 %collective-permute-start.35 = (f32[2,8,64,128]{3,2,1,0:T(8,128)S(1)}, f32[2,8,64,128]{3,2,1,0:T(8,128)S(1)}, u32[]{:S(2)}, u32[]{:S(2)}) collective-permute-start(f32[2,8,64,128]{3,2,1,0:T(8,128)S(1)} %get-tuple-element.223.own), channel_id=1, source_target_pairs={{0,8},{1,9},{2,10},{3,11},{4,12},{5,13},{6,14},{7,15},{8,0},{9,1},... | collective-permute-start | bytes 1572872 | tf_op jit(solution)/shard_map/ppermute | solution.py:22
  110.6 24.1 %collective-permute-start.23 = (f32[1,8,64,128]{3,2,1,0:T(8,128)S(1)}, f32[1,8,64,128]{3,2,1,0:T(8,128)S(1)}, u32[]{:S(2)}, u32[]{:S(2)}) collective-permute-start(f32[1,8,64,128]{3,2,1,0:T(8,128)S(1)} %get-tuple-element.203), channel_id=1, source_target_pairs={{0,80},{16,64},{32,112},{48,96},{64,16},{80,0},{96,48},{112,32},{1... | collective-permute-start | bytes 786440 | tf_op jit(solution)/shard_map/ppermute | solution.py:22
  117.2 19.1 %collective-permute-start.36 = (f32[2,8,64,128]{3,2,1,0:T(8,128)S(1)}, f32[2,8,64,128]{3,2,1,0:T(8,128)S(1)}, u32[]{:S(2)}, u32[]{:S(2)}) collective-permute-start(f32[2,8,64,128]{3,2,1,0:T(8,128)S(1)} %get-tuple-element.227.own), channel_id=1, source_target_pairs={{0,4},{1,5},{2,6},{3,7},{4,0},{5,1},{6,2},{7,3},{8,12},{9,13},{10,... | collective-permute-start | bytes 1572872 | tf_op jit(solution)/shard_map/ppermute | solution.py:22
  117.6 22.9 %collective-permute-start.34 = (f32[2,8,64,128]{3,2,1,0:T(8,128)S(1)}, f32[2,8,64,128]{3,2,1,0:T(8,128)S(1)}, u32[]{:S(2)}, u32[]{:S(2)}) collective-permute-start(f32[2,8,64,128]{3,2,1,0:T(8,128)S(1)} %get-tuple-element.222.own), channel_id=1, source_target_pairs={{0,8},{1,9},{2,10},{3,11},{4,12},{5,13},{6,14},{7,15},{8,0},{9,1},... | collective-permute-start | bytes 1572872 | tf_op jit(solution)/shard_map/ppermute | solution.py:22
  119.9 21.8 %collective-permute-start.37 = (f32[2,8,64,128]{3,2,1,0:T(8,128)S(1)}, f32[2,8,64,128]{3,2,1,0:T(8,128)S(1)}, u32[]{:S(2)}, u32[]{:S(2)}) collective-permute-start(f32[2,8,64,128]{3,2,1,0:T(8,128)S(1)} %get-tuple-element.231.own), channel_id=1, source_target_pairs={{0,2},{1,3},{2,0},{3,1},{4,6},{5,7},{6,4},{7,5},{8,10},{9,11},{10,... | collective-permute-start | bytes 1572872 | tf_op jit(solution)/shard_map/ppermute | solution.py:22
  134.8 17.0 %collective-permute-start.33 = (f32[2,8,64,128]{3,2,1,0:T(8,128)S(1)}, f32[2,8,64,128]{3,2,1,0:T(8,128)S(1)}, u32[]{:S(2)}, u32[]{:S(2)}) collective-permute-start(f32[2,8,64,128]{3,2,1,0:T(8,128)S(1)} %get-tuple-element.221.own), channel_id=1, source_target_pairs={{0,8},{1,9},{2,10},{3,11},{4,12},{5,13},{6,14},{7,15},{8,0},{9,1},... | collective-permute-start | bytes 1572872 | tf_op jit(solution)/shard_map/ppermute | solution.py:22
  135.0 21.1 %collective-permute-start.32 = (f32[2,8,64,128]{3,2,1,0:T(8,128)S(1)}, f32[2,8,64,128]{3,2,1,0:T(8,128)S(1)}, u32[]{:S(2)}, u32[]{:S(2)}) collective-permute-start(f32[2,8,64,128]{3,2,1,0:T(8,128)S(1)} %get-tuple-element.220.own), channel_id=1, source_target_pairs={{0,4},{1,5},{2,6},{3,7},{4,0},{5,1},{6,2},{7,3},{8,12},{9,13},{10,... | collective-permute-start | bytes 1572872 | tf_op jit(solution)/shard_map/ppermute | solution.py:22
  136.2 22.0 %collective-permute-start.31 = (f32[1,8,64,128]{3,2,1,0:T(8,128)S(1)}, f32[1,8,64,128]{3,2,1,0:T(8,128)S(1)}, u32[]{:S(2)}, u32[]{:S(2)}) collective-permute-start(f32[1,8,64,128]{3,2,1,0:T(8,128)S(1)} %get-tuple-element.219.own), channel_id=1, source_target_pairs={{0,2},{1,3},{2,0},{3,1},{4,6},{5,7},{6,4},{7,5},{8,10},{9,11},{10,... | collective-permute-start | bytes 786440 | tf_op jit(solution)/shard_map/ppermute | solution.py:22
  140.5 18.0 %collective-permute-start.30 = (f32[1,8,64,128]{3,2,1,0:T(8,128)S(1)}, f32[1,8,64,128]{3,2,1,0:T(8,128)S(1)}, u32[]{:S(2)}, u32[]{:S(2)}) collective-permute-start(f32[1,8,64,128]{3,2,1,0:T(8,128)S(1)} %get-tuple-element.218.own), channel_id=1, source_target_pairs={{0,1},{1,0},{2,3},{3,2},{4,5},{5,4},{6,7},{7,6},{8,9},{9,8},{10,11... | collective-permute-start | bytes 786440 | tf_op jit(solution)/shard_map/ppermute | solution.py:22
  141.8 22.9 %collective-permute-start.40 = (f32[2,8,64,128]{3,2,1,0:T(8,128)S(1)}, f32[2,8,64,128]{3,2,1,0:T(8,128)S(1)}, u32[]{:S(2)}, u32[]{:S(2)}) collective-permute-start(f32[2,8,64,128]{3,2,1,0:T(8,128)S(1)} %get-tuple-element.239.own), channel_id=1, source_target_pairs={{0,8},{1,9},{2,10},{3,11},{4,12},{5,13},{6,14},{7,15},{8,0},{9,1},... | collective-permute-start | bytes 1572872 | tf_op jit(solution)/shard_map/ppermute | solution.py:22
  151.7 21.2 %collective-permute-start.39 = (f32[2,8,64,128]{3,2,1,0:T(8,128)S(1)}, f32[2,8,64,128]{3,2,1,0:T(8,128)S(1)}, u32[]{:S(2)}, u32[]{:S(2)}) collective-permute-start(f32[2,8,64,128]{3,2,1,0:T(8,128)S(1)} %get-tuple-element.238.own), channel_id=1, source_target_pairs={{0,4},{1,5},{2,6},{3,7},{4,0},{5,1},{6,2},{7,3},{8,12},{9,13},{10,... | collective-permute-start | bytes 1572872 | tf_op jit(solution)/shard_map/ppermute | solution.py:22
  158.8 16.3 %collective-permute-start.38 = (f32[1,8,64,128]{3,2,1,0:T(8,128)S(1)}, f32[1,8,64,128]{3,2,1,0:T(8,128)S(1)}, u32[]{:S(2)}, u32[]{:S(2)}) collective-permute-start(f32[1,8,64,128]{3,2,1,0:T(8,128)S(1)} %get-tuple-element.237.own), channel_id=1, source_target_pairs={{0,2},{1,3},{2,0},{3,1},{4,6},{5,7},{6,4},{7,5},{8,10},{9,11},{10,... | collective-permute-start | bytes 786440 | tf_op jit(solution)/shard_map/ppermute | solution.py:22
  160.9 23.9 %collective-permute-start.42 = (f32[2,8,64,128]{3,2,1,0:T(8,128)S(1)}, f32[2,8,64,128]{3,2,1,0:T(8,128)S(1)}, u32[]{:S(2)}, u32[]{:S(2)}) collective-permute-start(f32[2,8,64,128]{3,2,1,0:T(8,128)S(1)} %get-tuple-element.245.own), channel_id=1, source_target_pairs={{0,8},{1,9},{2,10},{3,11},{4,12},{5,13},{6,14},{7,15},{8,0},{9,1},... | collective-permute-start | bytes 1572872 | tf_op jit(solution)/shard_map/ppermute | solution.py:22
  161.1 23.1 %collective-permute-start.43 = (f32[1,8,64,128]{3,2,1,0:T(8,128)S(1)}, f32[1,8,64,128]{3,2,1,0:T(8,128)S(1)}, u32[]{:S(2)}, u32[]{:S(2)}) collective-permute-start(f32[1,8,64,128]{3,2,1,0:T(8,128)S(1)} %get-tuple-element.247.own), channel_id=1, source_target_pairs={{0,4},{1,5},{2,6},{3,7},{4,0},{5,1},{6,2},{7,3},{8,12},{9,13},{10,... | collective-permute-start | bytes 786440 | tf_op jit(solution)/shard_map/ppermute | solution.py:22
  173.4 15.4 %collective-permute-start.46 = (f32[2,8,64,128]{3,2,1,0:T(8,128)S(1)}, f32[2,8,64,128]{3,2,1,0:T(8,128)S(1)}, u32[]{:S(2)}, u32[]{:S(2)}) collective-permute-start(f32[2,8,64,128]{3,2,1,0:T(8,128)S(1)} %get-tuple-element.253.own), channel_id=1, source_target_pairs={{0,8},{1,9},{2,10},{3,11},{4,12},{5,13},{6,14},{7,15},{8,0},{9,1},... | collective-permute-start | bytes 1572872 | tf_op jit(solution)/shard_map/ppermute | solution.py:22
  175.4 11.6 %collective-permute-start.41 = (f32[1,8,64,128]{3,2,1,0:T(8,128)S(1)}, f32[1,8,64,128]{3,2,1,0:T(8,128)S(1)}, u32[]{:S(2)}, u32[]{:S(2)}) collective-permute-start(f32[1,8,64,128]{3,2,1,0:T(8,128)S(1)} %get-tuple-element.244.own), channel_id=1, source_target_pairs={{0,4},{1,5},{2,6},{3,7},{4,0},{5,1},{6,2},{7,3},{8,12},{9,13},{10,... | collective-permute-start | bytes 786440 | tf_op jit(solution)/shard_map/ppermute | solution.py:22
  184.5 9.2 %collective-permute-start.45 = (f32[1,8,64,128]{3,2,1,0:T(8,128)S(1)}, f32[1,8,64,128]{3,2,1,0:T(8,128)S(1)}, u32[]{:S(2)}, u32[]{:S(2)}) collective-permute-start(f32[1,8,64,128]{3,2,1,0:T(8,128)S(1)} %get-tuple-element.252.own), channel_id=1, source_target_pairs={{0,8},{1,9},{2,10},{3,11},{4,12},{5,13},{6,14},{7,15},{8,0},{9,1},... | collective-permute-start | bytes 786440 | tf_op jit(solution)/shard_map/ppermute | solution.py:22
  187.3 9.3 %collective-permute-start.44 = (f32[1,8,64,128]{3,2,1,0:T(8,128)S(1)}, f32[1,8,64,128]{3,2,1,0:T(8,128)S(1)}, u32[]{:S(2)}, u32[]{:S(2)}) collective-permute-start(f32[1,8,64,128]{3,2,1,0:T(8,128)S(1)} %get-tuple-element.251.own), channel_id=1, source_target_pairs={{0,8},{1,9},{2,10},{3,11},{4,12},{5,13},{6,14},{7,15},{8,0},{9,1},... | collective-permute-start | bytes 786440 | tf_op jit(solution)/shard_map/ppermute | solution.py:22

commit v2 on v1

--- a/solution.py
+++ b/solution.py
@@ -226,14 +226,21 @@
 
 
 def last_body(chunk, parts, place, factors, own, other, *refs):
-    out, held, sem = refs[-4], refs[-2], refs[-1]
+    out, held, sems = refs[-4], refs[-2], refs[-1]
     first = (place[0] ^ chunk.part) * (factors.shape[1] // parts) + chunk.group
+    copies = []
     for slot in range(chunk.slots):
-        for group in range(chunk.groups):
-            factor = factors[chunk.slot + slot, first + group]
-            held[slot, group] = block_product(factor, own[slot, group], other[slot, group])
-    place_out = out.at[pl.ds(chunk.slot, chunk.slots), pl.ds(first, chunk.groups)]
-    run_copies([pltpu.make_async_copy(held, place_out, sem)])
+        for half in range(2):
+            begin, count = half * chunk.groups // 2, chunk.groups // 2
+            for group in range(begin, begin + count):
+                factor = factors[chunk.slot + slot, first + group]
+                held[slot, group] = block_product(factor, own[slot, group], other[slot, group])
+            target = out.at[chunk.slot + slot, pl.ds(first + begin, count)]
+            source = held.at[slot, pl.ds(begin, count)]
+            copies.append(pltpu.make_async_copy(source, target, sems.at[len(copies)]))
+            copies[-1].start()
+    for copy in copies:
+        copy.wait()
 
 
 def last_product(place, factors, own, other, chunk, parts, token, coeffs):
@@ -246,7 +253,7 @@
         [ANY],
         token,
         "last_product",
-        [pltpu.VMEM(own.shape, own.dtype), pltpu.SemaphoreType.DMA],
+        [pltpu.VMEM(own.shape, own.dtype), pltpu.SemaphoreType.DMA((2 * chunk.slots,))],
         {4: 0} if filled else {},
     )
 
@@ -259,9 +266,9 @@
     (LEND, 0), (PICK, 1), (LEND, 1), (PICK, 0), (PICK, 3), (PICK, 4), (LEND, 2), (PICK, 2), (BORROW, 0),
     (FETCH, 0), (ADMIT, 1), (0, 0), (PICK, 5), (BORROW, 1), (FETCH, 1), (ADMIT, 3), (0, 1), (1, 0),
     (ADMIT, 4), (ADMIT, 2), (FETCH, 3), (0, 3), (FETCH, 2), (BORROW, 2), (PICK, 6), (PICK, 8), (1, 1),
-    (ADMIT, 5), (2, 0), (0, 4), (1, 3), (0, 2), (3, 0), (1, 4), (2, 1), (ADMIT, 6), (0, 5), (1, 2), (PICK, 7),
-    (ADMIT, 8), (2, 3), (0, 6), (0, 8), (1, 5), (2, 2), (ADMIT, 7), (3, 1), (2, 4), (3, 3), (1, 6), (3, 2),
-    (2, 5), (1, 8), (0, 7), (3, 4), (2, 6), (1, 7), (2, 8), (3, 5), (2, 7), (3, 6), (3, 8), (3, 7),
+    (ADMIT, 5), (2, 0), (0, 4), (1, 3), (0, 2), (3, 0), (1, 4), (2, 1), (ADMIT, 6), (0, 5), (PICK, 7), (1, 2),
+    (ADMIT, 8), (2, 3), (3, 1), (0, 6), (1, 5), (ADMIT, 7), (2, 2), (2, 4), (3, 3), (0, 7), (1, 6), (3, 4),
+    (2, 5), (3, 2), (2, 6), (0, 8), (1, 7), (3, 5), (1, 8), (2, 7), (3, 6), (2, 8), (3, 7), (3, 8),
 )
 
 

time: 198 us -> 198 us (level)
  waiting for transfers between devices: 76.7 us -> 84.2 us
  starting transfers between devices: 70.9 us -> 63.5 us
    ppermute x47, waiting for transfers between devices: 76.7 us -> 84.2 us  [permute_xor(): lax.ppermute(x, axis, [(i, i ^ mask) for i in range(lax.axis_size(axis))])]
    ppermute x47, starting transfers between devices: 70.9 us -> 63.5 us  [permute_xor(): lax.ppermute(x, axis, [(i, i ^ mask) for i in range(lax.axis_size(axis))])]
  transfers between devices with their start and end apart: 47 -> 47, of which waited for: 22 -> 25; matrix products, arithmetic and copies ran while one was open for 0% -> 0% of each run, Pallas kernels for 24% -> 24%
where the time goes in v2:
time: 198 us; the launch traced here: 197 us
  waiting for transfers between devices  84.2 us (43%)
  starting transfers between devices  63.5 us (32%)
  Pallas kernels  48.5 us (24%)
    ppermute x47, waiting for transfers between devices, permute_xor(): lax.ppermute(x, axis, [(i, i ^ mask) for i in range(lax.axis_size(axis))])  84.2 us
    ppermute x47, starting transfers between devices, permute_xor(): lax.ppermute(x, axis, [(i, i ^ mask) for i in range(lax.axis_size(axis))])  63.5 us
    pallas_call x63, Pallas kernels, call(): pl.pallas_call(body, in_specs=in_specs + [ANY] * len(tokens), out_specs=o...  48.5 us
  transfers between devices with their start and end apart: 47, of which 25 were waited for; matrix products, arithmetic and copies ran while one was open for 0% of the time, Pallas kernels for 24%

profile of v2, /device:TPU:0, one launch (start us, length us, event | category | flops | bytes accessed | tf_op | source)
XLA Modules:
  0.0 196.9 jit_solution(10103072630676683872)
XLA Ops:
  1.1 2.1 %collective-permute-start.5 = (f32[2,8,64,128]{3,2,1,0:T(8,128)S(1)}, f32[2,8,64,128]{3,2,1,0:T(8,128)S(1)}, u32[]{:S(2)}, u32[]{:S(2)}) collective-permute-start(f32[2,8,64,128]{3,2,1,0:T(8,128)S(1)} %get-tuple-element.145), channel_id=1, source_target_pairs={{0,2},{1,3},{2,0},{3,1},{4,6},{5,7},{6,4},{7,5},{8,10},{9,11},{10,... | collective-permute-start | bytes 1572872 | tf_op jit(solution)/shard_map/ppermute | solution.py:22
  3.2 1.6 pick_slots.9
  4.8 1.7 collective-permute-start.4
  7.5 1.6 pick_slots.10
  9.4 1.6 pick_slots.11
  11.0 2.3 %collective-permute-start.8 = (f32[2,8,64,128]{3,2,1,0:T(8,128)S(1)}, f32[2,8,64,128]{3,2,1,0:T(8,128)S(1)}, u32[]{:S(2)}, u32[]{:S(2)}) collective-permute-start(f32[2,8,64,128]{3,2,1,0:T(8,128)S(1)} %get-tuple-element.158), channel_id=1, source_target_pairs={{0,96},{16,112},{32,64},{48,80},{64,32},{80,48},{96,0},{112,16},{1... | collective-permute-start | bytes 1572872 | tf_op jit(solution)/shard_map/ppermute | solution.py:22
  13.2 1.6 pick_slots.12
  15.9 1.6 pick_slots.13
  17.5 2.2 %fetch_factors.4 = (f32[2,64,64,128]{3,2,1,0:T(8,128)S(1)}, f32[8,128]{1,0:T(8,128)S(1)}) custom-call(f32[4,2,64,64,128]{4,3,2,1,0:T(8,128)} %factors.15, f32[8,128]{1,0:T(8,128)S(1)} %get-tuple-element.147.refs_0_), custom_call_target="tpu_custom_call" | custom-call | tf_op jit(solution)/shard_map/fetch_factors/pallas_call | solution.py:35
  21.4 2.0 %collective-permute-start.6 = (f32[2,8,64,128]{3,2,1,0:T(8,128)S(1)}, f32[2,8,64,128]{3,2,1,0:T(8,128)S(1)}, u32[]{:S(2)}, u32[]{:S(2)}) collective-permute-start(f32[2,8,64,128]{3,2,1,0:T(8,128)S(1)} %get-tuple-element.155.own), channel_id=1, source_target_pairs={{0,2},{1,3},{2,0},{3,1},{4,6},{5,7},{6,4},{7,5},{8,10},{9,11},{10,... | collective-permute-start | bytes 1572872 | tf_op jit(solution)/shard_map/ppermute | solution.py:22
  23.4 3.1 %collective-permute-start.1 = (f32[2,8,64,128]{3,2,1,0:T(8,128)S(1)}, f32[2,8,64,128]{3,2,1,0:T(8,128)S(1)}, u32[]{:S(2)}, u32[]{:S(2)}) collective-permute-start(f32[2,8,64,128]{3,2,1,0:T(8,128)S(1)} %get-tuple-element.141), channel_id=1, source_target_pairs={{0,48},{16,32},{32,16},{48,0},{64,112},{80,96},{96,80},{112,64},{1... | collective-permute-start | bytes 1572872 | tf_op jit(solution)/shard_map/ppermute | solution.py:22
  27.2 3.1 %collective-permute-start = (f32[2,8,64,128]{3,2,1,0:T(8,128)S(1)}, f32[2,8,64,128]{3,2,1,0:T(8,128)S(1)}, u32[]{:S(2)}, u32[]{:S(2)}) collective-permute-start(f32[2,8,64,128]{3,2,1,0:T(8,128)S(1)} %get-tuple-element.140), channel_id=1, source_target_pairs={{0,16},{16,0},{32,48},{48,32},{64,80},{80,64},{96,112},{112,96},{1... | collective-permute-start | bytes 1572872 | tf_op jit(solution)/shard_map/ppermute | solution.py:22
  30.3 1.6 pick_slots.14
  31.9 2.2 %fetch_factors.5 = (f32[2,64,64,128]{3,2,1,0:T(8,128)S(1)}, f32[8,128]{1,0:T(8,128)S(1)}) custom-call(f32[4,2,64,64,128]{4,3,2,1,0:T(8,128)} %factors.15, f32[8,128]{1,0:T(8,128)S(1)} %get-tuple-element.152.refs_0_), custom_call_target="tpu_custom_call" | custom-call | tf_op jit(solution)/shard_map/fetch_factors/pallas_call | solution.py:35
  34.3 2.0 %collective-permute-start.10 = (f32[2,8,64,128]{3,2,1,0:T(8,128)S(1)}, f32[2,8,64,128]{3,2,1,0:T(8,128)S(1)}, u32[]{:S(2)}, u32[]{:S(2)}) collective-permute-start(f32[2,8,64,128]{3,2,1,0:T(8,128)S(1)} %get-tuple-element.170), channel_id=1, source_target_pairs={{0,2},{1,3},{2,0},{3,1},{4,6},{5,7},{6,4},{7,5},{8,10},{9,11},{10,... | collective-permute-start | bytes 1572872 | tf_op jit(solution)/shard_map/ppermute | solution.py:22
  37.5 1.7 collective-permute-start.17
  40.5 2.7 %collective-permute-start.16 = (f32[2,8,64,128]{3,2,1,0:T(8,128)S(1)}, f32[2,8,64,128]{3,2,1,0:T(8,128)S(1)}, u32[]{:S(2)}, u32[]{:S(2)}) collective-permute-start(f32[2,8,64,128]{3,2,1,0:T(8,128)S(1)} %get-tuple-element.181), channel_id=1, source_target_pairs={{0,64},{16,80},{32,96},{48,112},{64,0},{80,16},{96,32},{112,48},{1... | collective-permute-start | bytes 1572872 | tf_op jit(solution)/shard_map/ppermute | solution.py:22
  43.3 7.0 %collective-permute-done.x = f32[2,8,64,128]{3,2,1,0:T(8,128)S(1)} collective-permute-done((f32[2,8,64,128]{3,2,1,0:T(8,128)S(1)}, f32[2,8,64,128]{3,2,1,0:T(8,128)S(1)}, u32[]{:S(2)}, u32[]{:S(2)}) %collective-permute-start) | collective-permute-done | bytes 524320 | tf_op jit(solution)/shard_map/ppermute | solution.py:22
  50.3 2.5 %collective-permute-start.15 = (f32[2,8,64,128]{3,2,1,0:T(8,128)S(1)}, f32[2,8,64,128]{3,2,1,0:T(8,128)S(1)}, u32[]{:S(2)}, u32[]{:S(2)}) collective-permute-start(f32[2,8,64,128]{3,2,1,0:T(8,128)S(1)} %get-tuple-element.180), channel_id=1, source_target_pairs={{0,6},{1,7},{2,4},{3,5},{4,2},{5,3},{6,0},{7,1},{8,14},{9,15},{10,... | collective-permute-start | bytes 1572872 | tf_op jit(solution)/shard_map/ppermute | solution.py:22
  52.8 2.2 %fetch_factors.6 = (f32[2,64,64,128]{3,2,1,0:T(8,128)S(1)}, f32[8,128]{1,0:T(8,128)S(1)}) custom-call(f32[4,2,64,64,128]{4,3,2,1,0:T(8,128)} %factors.15, f32[8,128]{1,0:T(8,128)S(1)} %get-tuple-element.164.refs_0_), custom_call_target="tpu_custom_call" | custom-call | tf_op jit(solution)/shard_map/fetch_factors/pallas_call | solution.py:35
  55.5 2.2 %fetch_factors.7 = (f32[2,64,64,128]{3,2,1,0:T(8,128)S(1)}, f32[8,128]{1,0:T(8,128)S(1)}) custom-call(f32[4,2,64,64,128]{4,3,2,1,0:T(8,128)} %factors.15, f32[8,128]{1,0:T(8,128)S(1)} %get-tuple-element.168.refs_0_), custom_call_target="tpu_custom_call" | custom-call | tf_op jit(solution)/shard_map/fetch_factors/pallas_call | solution.py:35
  57.7 1.6 pick_slots.15
  59.4 1.5 pick_slots.16
  62.9 1.8 collective-permute-done.15.other
  65.1 1.6 collective-permute-start.23
  67.8 2.4 %collective-permute-start.21 = (f32[2,8,64,128]{3,2,1,0:T(8,128)S(1)}, f32[2,8,64,128]{3,2,1,0:T(8,128)S(1)}, u32[]{:S(2)}, u32[]{:S(2)}) collective-permute-start(f32[2,8,64,128]{3,2,1,0:T(8,128)S(1)} %get-tuple-element.194), channel_id=1, source_target_pairs={{0,6},{1,7},{2,4},{3,5},{4,2},{5,3},{6,0},{7,1},{8,14},{9,15},{10,... | collective-permute-start | bytes 1572872 | tf_op jit(solution)/shard_map/ppermute | solution.py:22
  70.1 5.5 %collective-permute-done.13.other = f32[2,8,64,128]{3,2,1,0:T(8,128)S(1)} collective-permute-done((f32[2,8,64,128]{3,2,1,0:T(8,128)S(1)}, f32[2,8,64,128]{3,2,1,0:T(8,128)S(1)}, u32[]{:S(2)}, u32[]{:S(2)}) %collective-permute-start.13) | collective-permute-done | bytes 524320 | tf_op jit(solution)/shard_map/ppermute | solution.py:22
  75.7 4.1 %collective-permute-start.20 = (f32[2,8,64,128]{3,2,1,0:T(8,128)S(1)}, f32[2,8,64,128]{3,2,1,0:T(8,128)S(1)}, u32[]{:S(2)}, u32[]{:S(2)}) collective-permute-start(f32[2,8,64,128]{3,2,1,0:T(8,128)S(1)} %get-tuple-element.192), channel_id=1, source_target_pairs={{0,112},{16,96},{32,80},{48,64},{64,48},{80,32},{96,16},{112,0},{1... | collective-permute-start | bytes 1572872 | tf_op jit(solution)/shard_map/ppermute | solution.py:22
  81.7 5.2 %collective-permute-done.22.other = f32[2,8,64,128]{3,2,1,0:T(8,128)S(1)} collective-permute-done((f32[2,8,64,128]{3,2,1,0:T(8,128)S(1)}, f32[2,8,64,128]{3,2,1,0:T(8,128)S(1)}, u32[]{:S(2)}, u32[]{:S(2)}) %collective-permute-start.22) | collective-permute-done | bytes 524320 | tf_op jit(solution)/shard_map/ppermute | solution.py:22
  90.0 1.6 collective-permute-start.26
  92.4 3.8 %collective-permute-start.11 = (f32[1,8,64,128]{3,2,1,0:T(8,128)S(1)}, f32[1,8,64,128]{3,2,1,0:T(8,128)S(1)}, u32[]{:S(2)}, u32[]{:S(2)}) collective-permute-start(f32[1,8,64,128]{3,2,1,0:T(8,128)S(1)} %get-tuple-element.174), channel_id=1, source_target_pairs={{0,80},{16,64},{32,112},{48,96},{64,16},{80,0},{96,48},{112,32},{1... | collective-permute-start | bytes 786440 | tf_op jit(solution)/shard_map/ppermute | solution.py:22
  96.6 1.5 collective-permute-done.18.other
  101.4 11.2 %collective-permute-done.11.x = f32[1,8,64,128]{3,2,1,0:T(8,128)S(1)} collective-permute-done((f32[1,8,64,128]{3,2,1,0:T(8,128)S(1)}, f32[1,8,64,128]{3,2,1,0:T(8,128)S(1)}, u32[]{:S(2)}, u32[]{:S(2)}) %collective-permute-start.11) | collective-permute-done | bytes 262176 | tf_op jit(solution)/shard_map/ppermute | solution.py:22
  112.6 2.6 %collective-permute-start.34 = (f32[2,8,64,128]{3,2,1,0:T(8,128)S(1)}, f32[2,8,64,128]{3,2,1,0:T(8,128)S(1)}, u32[]{:S(2)}, u32[]{:S(2)}) collective-permute-start(f32[2,8,64,128]{3,2,1,0:T(8,128)S(1)} %get-tuple-element.223), channel_id=1, source_target_pairs={{0,6},{1,7},{2,4},{3,5},{4,2},{5,3},{6,0},{7,1},{8,14},{9,15},{10,... | collective-permute-start | bytes 1572872 | tf_op jit(solution)/shard_map/ppermute | solution.py:22
  115.6 1.7 collective-permute-start.29
  122.1 6.8 %collective-permute-done.29.x = f32[1,8,64,128]{3,2,1,0:T(8,128)S(1)} collective-permute-done((f32[1,8,64,128]{3,2,1,0:T(8,128)S(1)}, f32[1,8,64,128]{3,2,1,0:T(8,128)S(1)}, u32[]{:S(2)}, u32[]{:S(2)}) %collective-permute-start.29) | collective-permute-done | bytes 262176 | tf_op jit(solution)/shard_map/ppermute | solution.py:22
  128.8 8.1 %collective-permute-done.34.other = f32[2,8,64,128]{3,2,1,0:T(8,128)S(1)} collective-permute-done((f32[2,8,64,128]{3,2,1,0:T(8,128)S(1)}, f32[2,8,64,128]{3,2,1,0:T(8,128)S(1)}, u32[]{:S(2)}, u32[]{:S(2)}) %collective-permute-start.34) | collective-permute-done | bytes 524320 | tf_op jit(solution)/shard_map/ppermute | solution.py:22
  139.3 1.8 collective-permute-start.36
  143.6 1.8 collective-permute-start.35
  145.4 7.3 %collective-permute-done.37.other = f32[2,8,64,128]{3,2,1,0:T(8,128)S(1)} collective-permute-done((f32[2,8,64,128]{3,2,1,0:T(8,128)S(1)}, f32[2,8,64,128]{3,2,1,0:T(8,128)S(1)}, u32[]{:S(2)}, u32[]{:S(2)}) %collective-permute-start.37) | collective-permute-done | bytes 524320 | tf_op jit(solution)/shard_map/ppermute | solution.py:22
  154.9 1.8 collective-permute-start.40
  156.9 6.3 %collective-permute-done.36.other = f32[2,8,64,128]{3,2,1,0:T(8,128)S(1)} collective-permute-done((f32[2,8,64,128]{3,2,1,0:T(8,128)S(1)}, f32[2,8,64,128]{3,2,1,0:T(8,128)S(1)}, u32[]{:S(2)}, u32[]{:S(2)}) %collective-permute-start.36) | collective-permute-done | bytes 524320 | tf_op jit(solution)/shard_map/ppermute | solution.py:22
  168.5 2.8 %collective-permute-done.41.other = f32[1,8,64,128]{3,2,1,0:T(8,128)S(1)} collective-permute-done((f32[1,8,64,128]{3,2,1,0:T(8,128)S(1)}, f32[1,8,64,128]{3,2,1,0:T(8,128)S(1)}, u32[]{:S(2)}, u32[]{:S(2)}) %collective-permute-start.41) | collective-permute-done | bytes 262176 | tf_op jit(solution)/shard_map/ppermute | solution.py:22
  175.2 1.7 collective-permute-done.39.other
  178.5 4.8 %collective-permute-done.44.other = f32[1,8,64,128]{3,2,1,0:T(8,128)S(1)} collective-permute-done((f32[1,8,64,128]{3,2,1,0:T(8,128)S(1)}, f32[1,8,64,128]{3,2,1,0:T(8,128)S(1)}, u32[]{:S(2)}, u32[]{:S(2)}) %collective-permute-start.44) | collective-permute-done | bytes 262176 | tf_op jit(solution)/shard_map/ppermute | solution.py:22
  183.7 1.9 collective-permute-start.46
  188.1 1.6 collective-permute-start.45
  191.5 4.3 %collective-permute-done.45.other = f32[1,8,64,128]{3,2,1,0:T(8,128)S(1)} collective-permute-done((f32[1,8,64,128]{3,2,1,0:T(8,128)S(1)}, f32[1,8,64,128]{3,2,1,0:T(8,128)S(1)}, u32[]{:S(2)}, u32[]{:S(2)}) %collective-permute-start.45) | collective-permute-done | bytes 262176 | tf_op jit(solution)/shard_map/ppermute | solution.py:22
  (111 shorter events, 50.5 us)
Async XLA Ops:
  0.0 3.2 %copy-start = (s32[16]{0:T(128)S(1)}, s32[16]{0:T(128)}, u32[]{:S(2)}) copy-start(s32[16]{0:T(128)} %owner_map.17) | copy-start | bytes 196
  1.1 16.4 %collective-permute-start.5 = (f32[2,8,64,128]{3,2,1,0:T(8,128)S(1)}, f32[2,8,64,128]{3,2,1,0:T(8,128)S(1)}, u32[]{:S(2)}, u32[]{:S(2)}) collective-permute-start(f32[2,8,64,128]{3,2,1,0:T(8,128)S(1)} %get-tuple-element.145), channel_id=1, source_target_pairs={{0,2},{1,3},{2,0},{3,1},{4,6},{5,7},{6,4},{7,5},{8,10},{9,11},{10,... | collective-permute-start | bytes 1572872 | tf_op jit(solution)/shard_map/ppermute | solution.py:22
  4.8 15.0 %collective-permute-start.4 = (f32[2,8,64,128]{3,2,1,0:T(8,128)S(1)}, f32[2,8,64,128]{3,2,1,0:T(8,128)S(1)}, u32[]{:S(2)}, u32[]{:S(2)}) collective-permute-start(f32[2,8,64,128]{3,2,1,0:T(8,128)S(1)} %get-tuple-element.144), channel_id=1, source_target_pairs={{0,32},{16,48},{32,0},{48,16},{64,96},{80,112},{96,64},{112,80},{1... | collective-permute-start | bytes 1572872 | tf_op jit(solution)/shard_map/ppermute | solution.py:22
  9.1 10.8 %collective-permute-start.3 = (f32[2,8,64,128]{3,2,1,0:T(8,128)S(1)}, f32[2,8,64,128]{3,2,1,0:T(8,128)S(1)}, u32[]{:S(2)}, u32[]{:S(2)}) collective-permute-start(f32[2,8,64,128]{3,2,1,0:T(8,128)S(1)} %get-tuple-element.143.own), channel_id=1, source_target_pairs={{0,1},{1,0},{2,3},{3,2},{4,5},{5,4},{6,7},{7,6},{8,9},{9,8},{10,11... | collective-permute-start | bytes 1572872 | tf_op jit(solution)/shard_map/ppermute | solution.py:22
  9.2 18.0 %collective-permute-start.2 = (f32[2,8,64,128]{3,2,1,0:T(8,128)S(1)}, f32[2,8,64,128]{3,2,1,0:T(8,128)S(1)}, u32[]{:S(2)}, u32[]{:S(2)}) collective-permute-start(f32[2,8,64,128]{3,2,1,0:T(8,128)S(1)} %get-tuple-element.142), channel_id=1, source_target_pairs={{0,2},{1,3},{2,0},{3,1},{4,6},{5,7},{6,4},{7,5},{8,10},{9,11},{10,... | collective-permute-start | bytes 1572872 | tf_op jit(solution)/shard_map/ppermute | solution.py:22
  11.0 23.2 %collective-permute-start.8 = (f32[2,8,64,128]{3,2,1,0:T(8,128)S(1)}, f32[2,8,64,128]{3,2,1,0:T(8,128)S(1)}, u32[]{:S(2)}, u32[]{:S(2)}) collective-permute-start(f32[2,8,64,128]{3,2,1,0:T(8,128)S(1)} %get-tuple-element.158), channel_id=1, source_target_pairs={{0,96},{16,112},{32,64},{48,80},{64,32},{80,48},{96,0},{112,16},{1... | collective-permute-start | bytes 1572872 | tf_op jit(solution)/shard_map/ppermute | solution.py:22
  19.8 14.5 %collective-permute-start.7 = (f32[2,8,64,128]{3,2,1,0:T(8,128)S(1)}, f32[2,8,64,128]{3,2,1,0:T(8,128)S(1)}, u32[]{:S(2)}, u32[]{:S(2)}) collective-permute-start(f32[2,8,64,128]{3,2,1,0:T(8,128)S(1)} %get-tuple-element.157.own), channel_id=1, source_target_pairs={{0,1},{1,0},{2,3},{3,2},{4,5},{5,4},{6,7},{7,6},{8,9},{9,8},{10,11... | collective-permute-start | bytes 1572872 | tf_op jit(solution)/shard_map/ppermute | solution.py:22
  21.4 16.2 %collective-permute-start.6 = (f32[2,8,64,128]{3,2,1,0:T(8,128)S(1)}, f32[2,8,64,128]{3,2,1,0:T(8,128)S(1)}, u32[]{:S(2)}, u32[]{:S(2)}) collective-permute-start(f32[2,8,64,128]{3,2,1,0:T(8,128)S(1)} %get-tuple-element.155.own), channel_id=1, source_target_pairs={{0,2},{1,3},{2,0},{3,1},{4,6},{5,7},{6,4},{7,5},{8,10},{9,11},{10,... | collective-permute-start | bytes 1572872 | tf_op jit(solution)/shard_map/ppermute | solution.py:22
  23.4 17.2 %collective-permute-start.1 = (f32[2,8,64,128]{3,2,1,0:T(8,128)S(1)}, f32[2,8,64,128]{3,2,1,0:T(8,128)S(1)}, u32[]{:S(2)}, u32[]{:S(2)}) collective-permute-start(f32[2,8,64,128]{3,2,1,0:T(8,128)S(1)} %get-tuple-element.141), channel_id=1, source_target_pairs={{0,48},{16,32},{32,16},{48,0},{64,112},{80,96},{96,80},{112,64},{1... | collective-permute-start | bytes 1572872 | tf_op jit(solution)/shard_map/ppermute | solution.py:22
  27.2 23.1 %collective-permute-start = (f32[2,8,64,128]{3,2,1,0:T(8,128)S(1)}, f32[2,8,64,128]{3,2,1,0:T(8,128)S(1)}, u32[]{:S(2)}, u32[]{:S(2)}) collective-permute-start(f32[2,8,64,128]{3,2,1,0:T(8,128)S(1)} %get-tuple-element.140), channel_id=1, source_target_pairs={{0,16},{16,0},{32,48},{48,32},{64,80},{80,64},{96,112},{112,96},{1... | collective-permute-start | bytes 1572872 | tf_op jit(solution)/shard_map/ppermute | solution.py:22
  34.2 18.6 %collective-permute-start.9 = (f32[2,8,64,128]{3,2,1,0:T(8,128)S(1)}, f32[2,8,64,128]{3,2,1,0:T(8,128)S(1)}, u32[]{:S(2)}, u32[]{:S(2)}) collective-permute-start(f32[2,8,64,128]{3,2,1,0:T(8,128)S(1)} %get-tuple-element.166.own), channel_id=1, source_target_pairs={{0,1},{1,0},{2,3},{3,2},{4,5},{5,4},{6,7},{7,6},{8,9},{9,8},{10,11... | collective-permute-start | bytes 1572872 | tf_op jit(solution)/shard_map/ppermute | solution.py:22
  34.3 23.5 %collective-permute-start.10 = (f32[2,8,64,128]{3,2,1,0:T(8,128)S(1)}, f32[2,8,64,128]{3,2,1,0:T(8,128)S(1)}, u32[]{:S(2)}, u32[]{:S(2)}) collective-permute-start(f32[2,8,64,128]{3,2,1,0:T(8,128)S(1)} %get-tuple-element.170), channel_id=1, source_target_pairs={{0,2},{1,3},{2,0},{3,1},{4,6},{5,7},{6,4},{7,5},{8,10},{9,11},{10,... | collective-permute-start | bytes 1572872 | tf_op jit(solution)/shard_map/ppermute | solution.py:22
  37.5 24.4 %collective-permute-start.17 = (f32[2,8,64,128]{3,2,1,0:T(8,128)S(1)}, f32[2,8,64,128]{3,2,1,0:T(8,128)S(1)}, u32[]{:S(2)}, u32[]{:S(2)}) collective-permute-start(f32[2,8,64,128]{3,2,1,0:T(8,128)S(1)} %get-tuple-element.183.own), channel_id=1, source_target_pairs={{0,2},{1,3},{2,0},{3,1},{4,6},{5,7},{6,4},{7,5},{8,10},{9,11},{10,... | collective-permute-start | bytes 1572872 | tf_op jit(solution)/shard_map/ppermute | solution.py:22
  40.5 22.3 %collective-permute-start.16 = (f32[2,8,64,128]{3,2,1,0:T(8,128)S(1)}, f32[2,8,64,128]{3,2,1,0:T(8,128)S(1)}, u32[]{:S(2)}, u32[]{:S(2)}) collective-permute-start(f32[2,8,64,128]{3,2,1,0:T(8,128)S(1)} %get-tuple-element.181), channel_id=1, source_target_pairs={{0,64},{16,80},{32,96},{48,112},{64,0},{80,16},{96,32},{112,48},{1... | collective-permute-start | bytes 1572872 | tf_op jit(solution)/shard_map/ppermute | solution.py:22
  50.3 14.4 %collective-permute-start.15 = (f32[2,8,64,128]{3,2,1,0:T(8,128)S(1)}, f32[2,8,64,128]{3,2,1,0:T(8,128)S(1)}, u32[]{:S(2)}, u32[]{:S(2)}) collective-permute-start(f32[2,8,64,128]{3,2,1,0:T(8,128)S(1)} %get-tuple-element.180), channel_id=1, source_target_pairs={{0,6},{1,7},{2,4},{3,5},{4,2},{5,3},{6,0},{7,1},{8,14},{9,15},{10,... | collective-permute-start | bytes 1572872 | tf_op jit(solution)/shard_map/ppermute | solution.py:22
  52.8 13.9 %collective-permute-start.14 = (f32[2,8,64,128]{3,2,1,0:T(8,128)S(1)}, f32[2,8,64,128]{3,2,1,0:T(8,128)S(1)}, u32[]{:S(2)}, u32[]{:S(2)}) collective-permute-start(f32[2,8,64,128]{3,2,1,0:T(8,128)S(1)} %get-tuple-element.178.own), channel_id=1, source_target_pairs={{0,1},{1,0},{2,3},{3,2},{4,5},{5,4},{6,7},{7,6},{8,9},{9,8},{10,11... | collective-permute-start | bytes 1572872 | tf_op jit(solution)/shard_map/ppermute | solution.py:22
  60.9 14.8 %collective-permute-start.13 = (f32[2,8,64,128]{3,2,1,0:T(8,128)S(1)}, f32[2,8,64,128]{3,2,1,0:T(8,128)S(1)}, u32[]{:S(2)}, u32[]{:S(2)}) collective-permute-start(f32[2,8,64,128]{3,2,1,0:T(8,128)S(1)} %get-tuple-element.177.own), channel_id=1, source_target_pairs={{0,2},{1,3},{2,0},{3,1},{4,6},{5,7},{6,4},{7,5},{8,10},{9,11},{10,... | collective-permute-start | bytes 1572872 | tf_op jit(solution)/shard_map/ppermute | solution.py:22
  62.0 17.8 %collective-permute-start.12 = (f32[2,8,64,128]{3,2,1,0:T(8,128)S(1)}, f32[2,8,64,128]{3,2,1,0:T(8,128)S(1)}, u32[]{:S(2)}, u32[]{:S(2)}) collective-permute-start(f32[2,8,64,128]{3,2,1,0:T(8,128)S(1)} %get-tuple-element.176.own), channel_id=1, source_target_pairs={{0,1},{1,0},{2,3},{3,2},{4,5},{5,4},{6,7},{7,6},{8,9},{9,8},{10,11... | collective-permute-start | bytes 1572872 | tf_op jit(solution)/shard_map/ppermute | solution.py:22
  65.1 15.5 %collective-permute-start.23 = (f32[2,8,64,128]{3,2,1,0:T(8,128)S(1)}, f32[2,8,64,128]{3,2,1,0:T(8,128)S(1)}, u32[]{:S(2)}, u32[]{:S(2)}) collective-permute-start(f32[2,8,64,128]{3,2,1,0:T(8,128)S(1)} %get-tuple-element.196.own), channel_id=1, source_target_pairs={{0,8},{1,9},{2,10},{3,11},{4,12},{5,13},{6,14},{7,15},{8,0},{9,1},... | collective-permute-start | bytes 1572872 | tf_op jit(solution)/shard_map/ppermute | solution.py:22
  67.1 19.8 %collective-permute-start.22 = (f32[2,8,64,128]{3,2,1,0:T(8,128)S(1)}, f32[2,8,64,128]{3,2,1,0:T(8,128)S(1)}, u32[]{:S(2)}, u32[]{:S(2)}) collective-permute-start(f32[2,8,64,128]{3,2,1,0:T(8,128)S(1)} %get-tuple-element.195.own), channel_id=1, source_target_pairs={{0,2},{1,3},{2,0},{3,1},{4,6},{5,7},{6,4},{7,5},{8,10},{9,11},{10,... | collective-permute-start | bytes 1572872 | tf_op jit(solution)/shard_map/ppermute | solution.py:22
  67.8 21.8 %collective-permute-start.21 = (f32[2,8,64,128]{3,2,1,0:T(8,128)S(1)}, f32[2,8,64,128]{3,2,1,0:T(8,128)S(1)}, u32[]{:S(2)}, u32[]{:S(2)}) collective-permute-start(f32[2,8,64,128]{3,2,1,0:T(8,128)S(1)} %get-tuple-element.194), channel_id=1, source_target_pairs={{0,6},{1,7},{2,4},{3,5},{4,2},{5,3},{6,0},{7,1},{8,14},{9,15},{10,... | collective-permute-start | bytes 1572872 | tf_op jit(solution)/shard_map/ppermute | solution.py:22
  75.7 16.8 %collective-permute-start.20 = (f32[2,8,64,128]{3,2,1,0:T(8,128)S(1)}, f32[2,8,64,128]{3,2,1,0:T(8,128)S(1)}, u32[]{:S(2)}, u32[]{:S(2)}) collective-permute-start(f32[2,8,64,128]{3,2,1,0:T(8,128)S(1)} %get-tuple-element.192), channel_id=1, source_target_pairs={{0,112},{16,96},{32,80},{48,64},{64,48},{80,32},{96,16},{112,0},{1... | collective-permute-start | bytes 1572872 | tf_op jit(solution)/shard_map/ppermute | solution.py:22
  79.7 12.7 %collective-permute-start.19 = (f32[2,8,64,128]{3,2,1,0:T(8,128)S(1)}, f32[2,8,64,128]{3,2,1,0:T(8,128)S(1)}, u32[]{:S(2)}, u32[]{:S(2)}) collective-permute-start(f32[2,8,64,128]{3,2,1,0:T(8,128)S(1)} %get-tuple-element.191.own), channel_id=1, source_target_pairs={{0,1},{1,0},{2,3},{3,2},{4,5},{5,4},{6,7},{7,6},{8,9},{9,8},{10,11... | collective-permute-start | bytes 1572872 | tf_op jit(solution)/shard_map/ppermute | solution.py:22
  80.6 17.5 %collective-permute-start.18 = (f32[2,8,64,128]{3,2,1,0:T(8,128)S(1)}, f32[2,8,64,128]{3,2,1,0:T(8,128)S(1)}, u32[]{:S(2)}, u32[]{:S(2)}) collective-permute-start(f32[2,8,64,128]{3,2,1,0:T(8,128)S(1)} %get-tuple-element.190.own), channel_id=1, source_target_pairs={{0,2},{1,3},{2,0},{3,1},{4,6},{5,7},{6,4},{7,5},{8,10},{9,11},{10,... | collective-permute-start | bytes 1572872 | tf_op jit(solution)/shard_map/ppermute | solution.py:22
  86.9 28.2 %collective-permute-start.27 = (f32[2,8,64,128]{3,2,1,0:T(8,128)S(1)}, f32[2,8,64,128]{3,2,1,0:T(8,128)S(1)}, u32[]{:S(2)}, u32[]{:S(2)}) collective-permute-start(f32[2,8,64,128]{3,2,1,0:T(8,128)S(1)} %get-tuple-element.209.own), channel_id=1, source_target_pairs={{0,4},{1,5},{2,6},{3,7},{4,0},{5,1},{6,2},{7,3},{8,12},{9,13},{10,... | collective-permute-start | bytes 1572872 | tf_op jit(solution)/shard_map/ppermute | solution.py:22
  90.0 25.5 %collective-permute-start.26 = (f32[2,8,64,128]{3,2,1,0:T(8,128)S(1)}, f32[2,8,64,128]{3,2,1,0:T(8,128)S(1)}, u32[]{:S(2)}, u32[]{:S(2)}) collective-permute-start(f32[2,8,64,128]{3,2,1,0:T(8,128)S(1)} %get-tuple-element.207.own), channel_id=1, source_target_pairs={{0,8},{1,9},{2,10},{3,11},{4,12},{5,13},{6,14},{7,15},{8,0},{9,1},... | collective-permute-start | bytes 1572872 | tf_op jit(solution)/shard_map/ppermute | solution.py:22
  92.4 24.8 %collective-permute-start.25 = (f32[2,8,64,128]{3,2,1,0:T(8,128)S(1)}, f32[2,8,64,128]{3,2,1,0:T(8,128)S(1)}, u32[]{:S(2)}, u32[]{:S(2)}) collective-permute-start(f32[2,8,64,128]{3,2,1,0:T(8,128)S(1)} %get-tuple-element.206.own), channel_id=1, source_target_pairs={{0,1},{1,0},{2,3},{3,2},{4,5},{5,4},{6,7},{7,6},{8,9},{9,8},{10,11... | collective-permute-start | bytes 1572872 | tf_op jit(solution)/shard_map/ppermute | solution.py:22
  92.4 20.1 %collective-permute-start.11 = (f32[1,8,64,128]{3,2,1,0:T(8,128)S(1)}, f32[1,8,64,128]{3,2,1,0:T(8,128)S(1)}, u32[]{:S(2)}, u32[]{:S(2)}) collective-permute-start(f32[1,8,64,128]{3,2,1,0:T(8,128)S(1)} %get-tuple-element.174), channel_id=1, source_target_pairs={{0,80},{16,64},{32,112},{48,96},{64,16},{80,0},{96,48},{112,32},{1... | collective-permute-start | bytes 786440 | tf_op jit(solution)/shard_map/ppermute | solution.py:22
  98.1 22.5 %collective-permute-start.30 = (f32[2,8,64,128]{3,2,1,0:T(8,128)S(1)}, f32[2,8,64,128]{3,2,1,0:T(8,128)S(1)}, u32[]{:S(2)}, u32[]{:S(2)}) collective-permute-start(f32[2,8,64,128]{3,2,1,0:T(8,128)S(1)} %get-tuple-element.215.own), channel_id=1, source_target_pairs={{0,2},{1,3},{2,0},{3,1},{4,6},{5,7},{6,4},{7,5},{8,10},{9,11},{10,... | collective-permute-start | bytes 1572872 | tf_op jit(solution)/shard_map/ppermute | solution.py:22
  112.6 24.4 %collective-permute-start.34 = (f32[2,8,64,128]{3,2,1,0:T(8,128)S(1)}, f32[2,8,64,128]{3,2,1,0:T(8,128)S(1)}, u32[]{:S(2)}, u32[]{:S(2)}) collective-permute-start(f32[2,8,64,128]{3,2,1,0:T(8,128)S(1)} %get-tuple-element.223), channel_id=1, source_target_pairs={{0,6},{1,7},{2,4},{3,5},{4,2},{5,3},{6,0},{7,1},{8,14},{9,15},{10,... | collective-permute-start | bytes 1572872 | tf_op jit(solution)/shard_map/ppermute | solution.py:22
  115.1 22.2 %collective-permute-start.33 = (f32[2,8,64,128]{3,2,1,0:T(8,128)S(1)}, f32[2,8,64,128]{3,2,1,0:T(8,128)S(1)}, u32[]{:S(2)}, u32[]{:S(2)}) collective-permute-start(f32[2,8,64,128]{3,2,1,0:T(8,128)S(1)} %get-tuple-element.221.own), channel_id=1, source_target_pairs={{0,4},{1,5},{2,6},{3,7},{4,0},{5,1},{6,2},{7,3},{8,12},{9,13},{10,... | collective-permute-start | bytes 1572872 | tf_op jit(solution)/shard_map/ppermute | solution.py:22
  115.6 13.2 %collective-permute-start.29 = (f32[1,8,64,128]{3,2,1,0:T(8,128)S(1)}, f32[1,8,64,128]{3,2,1,0:T(8,128)S(1)}, u32[]{:S(2)}, u32[]{:S(2)}) collective-permute-start(f32[1,8,64,128]{3,2,1,0:T(8,128)S(1)} %get-tuple-element.214), channel_id=1, source_target_pairs={{0,80},{16,64},{32,112},{48,96},{64,16},{80,0},{96,48},{112,32},{1... | collective-permute-start | bytes 786440 | tf_op jit(solution)/shard_map/ppermute | solution.py:22
  117.3 22.1 %collective-permute-start.32 = (f32[2,8,64,128]{3,2,1,0:T(8,128)S(1)}, f32[2,8,64,128]{3,2,1,0:T(8,128)S(1)}, u32[]{:S(2)}, u32[]{:S(2)}) collective-permute-start(f32[2,8,64,128]{3,2,1,0:T(8,128)S(1)} %get-tuple-element.219.own), channel_id=1, source_target_pairs={{0,8},{1,9},{2,10},{3,11},{4,12},{5,13},{6,14},{7,15},{8,0},{9,1},... | collective-permute-start | bytes 1572872 | tf_op jit(solution)/shard_map/ppermute | solution.py:22
  120.6 22.5 %collective-permute-start.28 = (f32[2,8,64,128]{3,2,1,0:T(8,128)S(1)}, f32[2,8,64,128]{3,2,1,0:T(8,128)S(1)}, u32[]{:S(2)}, u32[]{:S(2)}) collective-permute-start(f32[2,8,64,128]{3,2,1,0:T(8,128)S(1)} %get-tuple-element.213.own), channel_id=1, source_target_pairs={{0,2},{1,3},{2,0},{3,1},{4,6},{5,7},{6,4},{7,5},{8,10},{9,11},{10,... | collective-permute-start | bytes 1572872 | tf_op jit(solution)/shard_map/ppermute | solution.py:22
  128.8 13.5 %collective-permute-start.31 = (f32[1,8,64,128]{3,2,1,0:T(8,128)S(1)}, f32[1,8,64,128]{3,2,1,0:T(8,128)S(1)}, u32[]{:S(2)}, u32[]{:S(2)}) collective-permute-start(f32[1,8,64,128]{3,2,1,0:T(8,128)S(1)} %get-tuple-element.218.own), channel_id=1, source_target_pairs={{0,1},{1,0},{2,3},{3,2},{4,5},{5,4},{6,7},{7,6},{8,9},{9,8},{10,11... | collective-permute-start | bytes 786440 | tf_op jit(solution)/shard_map/ppermute | solution.py:22
  137.8 14.9 %collective-permute-start.37 = (f32[2,8,64,128]{3,2,1,0:T(8,128)S(1)}, f32[2,8,64,128]{3,2,1,0:T(8,128)S(1)}, u32[]{:S(2)}, u32[]{:S(2)}) collective-permute-start(f32[2,8,64,128]{3,2,1,0:T(8,128)S(1)} %get-tuple-element.231.own), channel_id=1, source_target_pairs={{0,8},{1,9},{2,10},{3,11},{4,12},{5,13},{6,14},{7,15},{8,0},{9,1},... | collective-permute-start | bytes 1572872 | tf_op jit(solution)/shard_map/ppermute | solution.py:22
  138.1 16.4 %collective-permute-start.38 = (f32[2,8,64,128]{3,2,1,0:T(8,128)S(1)}, f32[2,8,64,128]{3,2,1,0:T(8,128)S(1)}, u32[]{:S(2)}, u32[]{:S(2)}) collective-permute-start(f32[2,8,64,128]{3,2,1,0:T(8,128)S(1)} %get-tuple-element.235.own), channel_id=1, source_target_pairs={{0,4},{1,5},{2,6},{3,7},{4,0},{5,1},{6,2},{7,3},{8,12},{9,13},{10,... | collective-permute-start | bytes 1572872 | tf_op jit(solution)/shard_map/ppermute | solution.py:22
  139.3 23.9 %collective-permute-start.36 = (f32[2,8,64,128]{3,2,1,0:T(8,128)S(1)}, f32[2,8,64,128]{3,2,1,0:T(8,128)S(1)}, u32[]{:S(2)}, u32[]{:S(2)}) collective-permute-start(f32[2,8,64,128]{3,2,1,0:T(8,128)S(1)} %get-tuple-element.230.own), channel_id=1, source_target_pairs={{0,8},{1,9},{2,10},{3,11},{4,12},{5,13},{6,14},{7,15},{8,0},{9,1},... | collective-permute-start | bytes 1572872 | tf_op jit(solution)/shard_map/ppermute | solution.py:22
  143.6 22.2 %collective-permute-start.35 = (f32[2,8,64,128]{3,2,1,0:T(8,128)S(1)}, f32[2,8,64,128]{3,2,1,0:T(8,128)S(1)}, u32[]{:S(2)}, u32[]{:S(2)}) collective-permute-start(f32[2,8,64,128]{3,2,1,0:T(8,128)S(1)} %get-tuple-element.229.own), channel_id=1, source_target_pairs={{0,4},{1,5},{2,6},{3,7},{4,0},{5,1},{6,2},{7,3},{8,12},{9,13},{10,... | collective-permute-start | bytes 1572872 | tf_op jit(solution)/shard_map/ppermute | solution.py:22
  145.4 20.8 %collective-permute-start.24 = (f32[1,8,64,128]{3,2,1,0:T(8,128)S(1)}, f32[1,8,64,128]{3,2,1,0:T(8,128)S(1)}, u32[]{:S(2)}, u32[]{:S(2)}) collective-permute-start(f32[1,8,64,128]{3,2,1,0:T(8,128)S(1)} %get-tuple-element.205.own), channel_id=1, source_target_pairs={{0,1},{1,0},{2,3},{3,2},{4,5},{5,4},{6,7},{7,6},{8,9},{9,8},{10,11... | collective-permute-start | bytes 786440 | tf_op jit(solution)/shard_map/ppermute | solution.py:22
  154.9 19.1 %collective-permute-start.40 = (f32[2,8,64,128]{3,2,1,0:T(8,128)S(1)}, f32[2,8,64,128]{3,2,1,0:T(8,128)S(1)}, u32[]{:S(2)}, u32[]{:S(2)}) collective-permute-start(f32[2,8,64,128]{3,2,1,0:T(8,128)S(1)} %get-tuple-element.241.own), channel_id=1, source_target_pairs={{0,8},{1,9},{2,10},{3,11},{4,12},{5,13},{6,14},{7,15},{8,0},{9,1},... | collective-permute-start | bytes 1572872 | tf_op jit(solution)/shard_map/ppermute | solution.py:22
  156.8 14.4 %collective-permute-start.41 = (f32[1,8,64,128]{3,2,1,0:T(8,128)S(1)}, f32[1,8,64,128]{3,2,1,0:T(8,128)S(1)}, u32[]{:S(2)}, u32[]{:S(2)}) collective-permute-start(f32[1,8,64,128]{3,2,1,0:T(8,128)S(1)} %get-tuple-element.243.own), channel_id=1, source_target_pairs={{0,2},{1,3},{2,0},{3,1},{4,6},{5,7},{6,4},{7,5},{8,10},{9,11},{10,... | collective-permute-start | bytes 786440 | tf_op jit(solution)/shard_map/ppermute | solution.py:22
  166.5 10.4 %collective-permute-start.39 = (f32[1,8,64,128]{3,2,1,0:T(8,128)S(1)}, f32[1,8,64,128]{3,2,1,0:T(8,128)S(1)}, u32[]{:S(2)}, u32[]{:S(2)}) collective-permute-start(f32[1,8,64,128]{3,2,1,0:T(8,128)S(1)} %get-tuple-element.240.own), channel_id=1, source_target_pairs={{0,2},{1,3},{2,0},{3,1},{4,6},{5,7},{6,4},{7,5},{8,10},{9,11},{10,... | collective-permute-start | bytes 786440 | tf_op jit(solution)/shard_map/ppermute | solution.py:22
  167.0 18.6 %collective-permute-start.43 = (f32[2,8,64,128]{3,2,1,0:T(8,128)S(1)}, f32[2,8,64,128]{3,2,1,0:T(8,128)S(1)}, u32[]{:S(2)}, u32[]{:S(2)}) collective-permute-start(f32[2,8,64,128]{3,2,1,0:T(8,128)S(1)} %get-tuple-element.248.own), channel_id=1, source_target_pairs={{0,8},{1,9},{2,10},{3,11},{4,12},{5,13},{6,14},{7,15},{8,0},{9,1},... | collective-permute-start | bytes 1572872 | tf_op jit(solution)/shard_map/ppermute | solution.py:22
  171.5 11.9 %collective-permute-start.44 = (f32[1,8,64,128]{3,2,1,0:T(8,128)S(1)}, f32[1,8,64,128]{3,2,1,0:T(8,128)S(1)}, u32[]{:S(2)}, u32[]{:S(2)}) collective-permute-start(f32[1,8,64,128]{3,2,1,0:T(8,128)S(1)} %get-tuple-element.250.own), channel_id=1, source_target_pairs={{0,4},{1,5},{2,6},{3,7},{4,0},{5,1},{6,2},{7,3},{8,12},{9,13},{10,... | collective-permute-start | bytes 786440 | tf_op jit(solution)/shard_map/ppermute | solution.py:22
  177.1 10.7 %collective-permute-start.42 = (f32[1,8,64,128]{3,2,1,0:T(8,128)S(1)}, f32[1,8,64,128]{3,2,1,0:T(8,128)S(1)}, u32[]{:S(2)}, u32[]{:S(2)}) collective-permute-start(f32[1,8,64,128]{3,2,1,0:T(8,128)S(1)} %get-tuple-element.247.own), channel_id=1, source_target_pairs={{0,4},{1,5},{2,6},{3,7},{4,0},{5,1},{6,2},{7,3},{8,12},{9,13},{10,... | collective-permute-start | bytes 786440 | tf_op jit(solution)/shard_map/ppermute | solution.py:22
  183.7 6.8 %collective-permute-start.46 = (f32[1,8,64,128]{3,2,1,0:T(8,128)S(1)}, f32[1,8,64,128]{3,2,1,0:T(8,128)S(1)}, u32[]{:S(2)}, u32[]{:S(2)}) collective-permute-start(f32[1,8,64,128]{3,2,1,0:T(8,128)S(1)} %get-tuple-element.255.own), channel_id=1, source_target_pairs={{0,8},{1,9},{2,10},{3,11},{4,12},{5,13},{6,14},{7,15},{8,0},{9,1},... | collective-permute-start | bytes 786440 | tf_op jit(solution)/shard_map/ppermute | solution.py:22
  188.1 7.6 %collective-permute-start.45 = (f32[1,8,64,128]{3,2,1,0:T(8,128)S(1)}, f32[1,8,64,128]{3,2,1,0:T(8,128)S(1)}, u32[]{:S(2)}, u32[]{:S(2)}) collective-permute-start(f32[1,8,64,128]{3,2,1,0:T(8,128)S(1)} %get-tuple-element.254.own), channel_id=1, source_target_pairs={{0,8},{1,9},{2,10},{3,11},{4,12},{5,13},{6,14},{7,15},{8,0},{9,1},... | collective-permute-start | bytes 786440 | tf_op jit(solution)/shard_map/ppermute | solution.py:22
